TPU v7x, 32 devices: a whole 2x2x4 slice. The times are simulated.
32 devices in a mesh: edge: 16 (over z, y, x), rep: 2 (over core).
Axes of the slice: x: 2, y: 2, z: 4, core: 2. Of those that a mesh axis runs over, the one named last changes fastest.
Arguments:
- nodes: bfloat16 [64, 131072], P(None, ('edge', 'rep')), may hold values from -6 to 6
- edges: bfloat16 [64, 524288], P(None, ('edge', 'rep')), may hold values from -6 to 6
- target: bfloat16 [64, 131072], P(None, ('edge', 'rep')), may hold values from -6 to 6
- senders: int32 [524288], P(('edge', 'rep')), may hold values from 0 to 4095
- receivers: int32 [524288], P(('edge', 'rep')), may hold values from 0 to 4095
- counts: int32 [512], P(('edge', 'rep')), may hold values from 1 to 1024, as said below
- levels: int32 [131072], P(('edge', 'rep')), may hold values from 0 to 3
- land: int32 [131072], P(('edge', 'rep')), may hold values 0 or 1
- channel_mask: int32 [4, 64], replicated, may hold values 0 or 1
- edge_in: bfloat16 [192, 64], replicated, may hold values from -0.4375 to 0.4375
- edge_in_bias: bfloat16 [64], replicated, may hold values from -3 to 3
- edge_out: bfloat16 [64, 64], replicated, may hold values from -0.75 to 0.75
- edge_out_bias: bfloat16 [64], replicated, may hold values from -3 to 3
- edge_gain: bfloat16 [64], replicated, may hold values from 0.25 to 1.75
- edge_shift: bfloat16 [64], replicated, may hold values from -3 to 3
- node_in: bfloat16 [128, 64], replicated, may hold values from -0.5 to 0.5
- node_in_bias: bfloat16 [64], replicated, may hold values from -3 to 3
- node_out: bfloat16 [64, 64], replicated, may hold values from -0.75 to 0.75
- node_out_bias: bfloat16 [64], replicated, may hold values from -3 to 3
- node_gain: bfloat16 [64], replicated, may hold values from 0.25 to 1.75
- node_shift: bfloat16 [64], replicated, may hold values from -3 to 3
Outputs:
- new_nodes: bfloat16 [64, 131072], P(None, ('edge', 'rep'))
- node_grad: bfloat16 [64, 131072], P(None, ('edge', 'rep'))
- edge_grad: bfloat16 [64, 524288], P(None, ('edge', 'rep'))
- edge_in_grad: float32 [192, 64], replicated
- edge_in_bias_grad: float32 [64], replicated
- edge_out_grad: float32 [64, 64], replicated
- edge_out_bias_grad: float32 [64], replicated
- edge_gain_grad: float32 [64], replicated
- edge_shift_grad: float32 [64], replicated
- node_in_grad: float32 [128, 64], replicated
- node_in_bias_grad: float32 [64], replicated
- node_out_grad: float32 [64, 64], replicated
- node_out_bias_grad: float32 [64], replicated
- node_gain_grad: float32 [64], replicated
- node_shift_grad: float32 [64], replicated
Inputs may be any that keep to these rules, and one draw needn't show every extreme that they name: `counts`: in every draw some owner gets 1024 live slots from every sender block of its region, and another gets exactly 1 from every one.
All inputs are finite; a program needn't handle non-finite values. No bound on the sum of `land` on one device may be relied on, other than what follows from the above.
Results may differ from a plain program's by a relative error of at most 0.0081.
Values may be sent and summed in bfloat16 or wider, within the bound.
A program may use at most 128 MiB of HBM per device.

v0:
```python
import math

import jax
import jax.numpy as jnp
from jax import lax
from jax.sharding import PartitionSpec as P

NORM_EPS = 1e-05


def contract_rows(weight, columns):
    return lax.dot_general(
        weight, columns, (((0,), (0,)), ((), ())), preferred_element_type=jnp.float32
    )


def apply_rows(weight, columns):
    return lax.dot_general(
        weight, columns, (((1,), (0,)), ((), ())), preferred_element_type=jnp.float32
    )


def outer_sum(left, right):
    return lax.dot_general(
        left, right, (((1,), (1,)), ((), ())), preferred_element_type=jnp.float32
    )


def norm_forward(values, gain, shift):
    center = jnp.mean(values, axis=0, keepdims=True)
    shifted = values - center
    inverse = lax.rsqrt(jnp.mean(shifted * shifted, axis=0, keepdims=True) + NORM_EPS)
    normal = shifted * inverse
    return (
        normal * gain.astype(jnp.float32)[:, None] + shift.astype(jnp.float32)[:, None],
        normal,
        inverse,
    )


def norm_backward(grad, normal, inverse, gain):
    scaled = grad * gain.astype(jnp.float32)[:, None]
    gain_grad = jnp.sum(grad * normal, axis=1)
    shift_grad = jnp.sum(grad, axis=1)
    value_grad = inverse * (
        scaled
        - jnp.mean(scaled, axis=0, keepdims=True)
        - normal * jnp.mean(scaled * normal, axis=0, keepdims=True)
    )
    return (value_grad, gain_grad, shift_grad)


def silu_slope(values):
    logistic = jax.nn.sigmoid(values)
    return logistic * (1.0 + values * (1.0 - logistic))


def segment_columns(values, node_ids, node_count):
    block_len = math.gcd(values.shape[1], 2048)
    turns = values.shape[1] // block_len
    node_iota = lax.broadcasted_iota(jnp.int32, (block_len, node_count), 1)

    def advance(turn_index, running):
        offset = turn_index * block_len
        piece_cols = lax.dynamic_slice_in_dim(values, offset, block_len, 1)
        slot_ids = lax.dynamic_slice_in_dim(node_ids, offset, block_len, 0)
        one_hot = (slot_ids[:, None] == node_iota).astype(jnp.bfloat16)
        return running + jnp.dot(piece_cols, one_hot, preferred_element_type=jnp.float32)

    return lax.fori_loop(0, turns, advance, jnp.zeros((values.shape[0], node_count), jnp.float32))


def branch_forward(stacked, w_first, b_first, w_second, b_second, gain, shift):
    pre_act = contract_rows(w_first, stacked) + b_first.astype(jnp.float32)[:, None]
    hidden = jax.nn.silu(pre_act).astype(jnp.bfloat16)
    outer = contract_rows(w_second, hidden) + b_second.astype(jnp.float32)[:, None]
    normed, normal, inverse = norm_forward(outer, gain, shift)
    return (normed, (stacked, pre_act, hidden, normal, inverse))


def branch_backward(grad, saved, w_first, w_second, gain):
    stacked, pre_act, hidden, normal, inverse = saved
    outer_grad, gain_grad, shift_grad = norm_backward(grad, normal, inverse, gain)
    outer_low = outer_grad.astype(jnp.bfloat16)
    second_grad = outer_sum(hidden, outer_low)
    second_bias_grad = jnp.sum(outer_low.astype(jnp.float32), axis=1)
    pre_grad = (apply_rows(w_second, outer_low) * silu_slope(pre_act)).astype(jnp.bfloat16)
    first_grad = outer_sum(stacked, pre_grad)
    first_bias_grad = jnp.sum(pre_grad.astype(jnp.float32), axis=1)
    stacked_grad = apply_rows(w_first, pre_grad)
    return (
        stacked_grad,
        (first_grad, first_bias_grad, second_grad, second_bias_grad, gain_grad, shift_grad),
    )


def per_device(
    nodes,
    edges,
    target,
    senders,
    receivers,
    counts,
    levels,
    land,
    channel_mask,
    edge_in,
    edge_in_bias,
    edge_out,
    edge_out_bias,
    edge_gain,
    edge_shift,
    node_in,
    node_in_bias,
    node_out,
    node_out_bias,
    node_gain,
    node_shift,
):
    feature_rows = nodes.shape[0]
    node_count = nodes.shape[1]
    slot_count = edges.shape[1]
    capacity = slot_count // lax.axis_size("edge")
    position = jnp.arange(slot_count, dtype=jnp.int32) % capacity
    sender_live = (position < jnp.repeat(counts, capacity)).astype(jnp.float32)
    sender_cols = jnp.take(nodes, senders, axis=1)
    owner_rows = jnp.take(nodes, receivers, axis=1)
    receiver_cols = lax.all_to_all(owner_rows, "edge", split_axis=1, concat_axis=1, tiled=True)
    stacked = jnp.concatenate([edges, sender_cols, receiver_cols], axis=0)
    normed, saved = branch_forward(
        stacked, edge_in, edge_in_bias, edge_out, edge_out_bias, edge_gain, edge_shift
    )
    message = ((edges.astype(jnp.float32) + normed) * sender_live[None, :]).astype(jnp.bfloat16)
    message, saved = (message, saved)
    arrived = lax.all_to_all(message, "edge", split_axis=1, concat_axis=1, tiled=True)
    stacked = jnp.concatenate(
        [nodes, segment_columns(arrived, receivers, node_count).astype(jnp.bfloat16)], axis=0
    )
    normed, node_saved = branch_forward(
        stacked, node_in, node_in_bias, node_out, node_out_bias, node_gain, node_shift
    )
    state = nodes.astype(jnp.float32) + normed
    level_hot = (
        levels[None, :] == jnp.arange(channel_mask.shape[0], dtype=jnp.int32)[:, None]
    ).astype(jnp.float32)
    loss_weight = (
        jnp.dot(channel_mask.astype(jnp.float32).T, level_hot) * land.astype(jnp.float32)[None, :]
    )
    state_grad = loss_weight * (state - target.astype(jnp.float32))
    stacked_grad, node_grads = branch_backward(state_grad, node_saved, node_in, node_out, node_gain)
    node_part = state_grad + stacked_grad[:feature_rows]
    aggregate_grad = stacked_grad[feature_rows:].astype(jnp.bfloat16)
    new_nodes, node_part, owner_grad, node_grads = (
        state.astype(jnp.bfloat16),
        node_part,
        jnp.take(aggregate_grad, receivers, axis=1),
        node_grads,
    )
    message_grad = lax.all_to_all(owner_grad, "edge", split_axis=1, concat_axis=1, tiled=True)
    updated_grad = message_grad.astype(jnp.float32) * sender_live[None, :]
    stacked_grad, edge_grads = branch_backward(updated_grad, saved, edge_in, edge_out, edge_gain)
    edge_part = updated_grad + stacked_grad[:feature_rows]
    sender_part = stacked_grad[feature_rows : 2 * feature_rows].astype(jnp.bfloat16)
    receiver_part = stacked_grad[2 * feature_rows :].astype(jnp.bfloat16)
    edge_part, sender_grad, receiver_grad, edge_grads = (
        edge_part,
        sender_part,
        receiver_part,
        edge_grads,
    )
    returned = lax.all_to_all(receiver_grad, "edge", split_axis=1, concat_axis=1, tiled=True)
    edge_grad = edge_part.astype(jnp.bfloat16)
    node_total = (
        node_part
        + segment_columns(sender_grad, senders, node_count)
        + segment_columns(returned, receivers, node_count)
    )
    edge_first, edge_first_bias, edge_second, edge_second_bias, edge_gain_part, edge_shift_part = (
        edge_grads
    )
    node_first, node_first_bias, node_second, node_second_bias, node_gain_part, node_shift_part = (
        node_grads
    )
    summed_grads = lax.psum(
        (
            edge_first,
            edge_first_bias,
            edge_second,
            edge_second_bias,
            edge_gain_part,
            edge_shift_part,
            node_first,
            node_first_bias,
            node_second,
            node_second_bias,
            node_gain_part,
            node_shift_part,
        ),
        ("edge", "rep"),
    )
    return (
        new_nodes,
        node_total.astype(jnp.bfloat16),
        edge_grad,
        summed_grads[0],
        summed_grads[1],
        summed_grads[2],
        summed_grads[3],
        summed_grads[4],
        summed_grads[5],
        summed_grads[6],
        summed_grads[7],
        summed_grads[8],
        summed_grads[9],
        summed_grads[10],
        summed_grads[11],
    )


def solution(mesh):
    placed = (
        P(None, ("edge", "rep")),
        P(None, ("edge", "rep")),
        P(None, ("edge", "rep")),
        P(("edge", "rep")),
        P(("edge", "rep")),
        P(("edge", "rep")),
        P(("edge", "rep")),
        P(("edge", "rep")),
        P(),
        P(),
        P(),
        P(),
        P(),
        P(),
        P(),
        P(),
        P(),
        P(),
        P(),
        P(),
        P(),
    )
    return jax.shard_map(
        per_device,
        mesh=mesh,
        in_specs=placed,
        out_specs=(
            P(None, ("edge", "rep")),
            P(None, ("edge", "rep")),
            P(None, ("edge", "rep")),
            P(),
            P(),
            P(),
            P(),
            P(),
            P(),
            P(),
            P(),
            P(),
            P(),
            P(),
            P(),
        ),
        check_vma=False,
    )
```

profile of v0, /device:TPU:0, one launch (start us, length us, event | category | flops | bytes accessed | tf_op | source)
XLA Modules:
  0.0 721.7 jit_solution(2388086812783792136)
XLA Ops:
  10.5 57.4 %gather_fusion.1 = bf16[16384,64]{1,0:T(8,128)(2,1)} fusion(bf16[64,4096]{0,1:T(8,128)(2,1)S(1)} %copy.51, s32[16384]{0:T(1024)S(1)} %fusion.65), kind=kCustom, calls=%fused_computation.1.clone | custom fusion | bytes 4259840 | tf_op jit(solution)/shard_map/jit(_take)/gather | solution.py:127
  67.9 11.5 %broadcast_select_fusion.1 = bf16[16384,64]{1,0:T(8,128)(2,1)} fusion(bf16[16384,64]{1,0:T(8,128)(2,1)} %gather_fusion.1, pred[16384]{0:T(1024)(128)(4,1)S(1)} %compare_and_fusion), kind=kLoop, calls=%fused_computation.69 | loop fusion | flops 1048576 | bytes 4210688 | tf_op jit(solution)/shard_map/jit(_take)/select_n | solution.py:127
  79.4 4.8 copy.53
  84.2 8.4 %all-to-all-start = ((bf16[64,16,1024]{2,0,1:T(8,128)(2,1)}), bf16[64,16,1024]{2,0,1:T(8,128)(2,1)}, u32[]{:S(2)}, u32[]{:S(2)}) async-start(bf16[64,16,1024]{2,0,1:T(8,128)(2,1)} %copy.53), calls=%async_computation | async-start | bytes 4194304 | tf_op jit(solution)/shard_map/all_to_all | solution.py:128
  92.9 57.4 %gather_fusion = bf16[16384,64]{1,0:T(8,128)(2,1)} fusion(bf16[64,4096]{0,1:T(8,128)(2,1)S(1)} %copy.51, s32[16384]{0:T(1024)S(1)} %fusion.64), kind=kCustom, calls=%fused_computation.clone | custom fusion | bytes 4259840 | tf_op jit(solution)/shard_map/jit(_take)/gather | solution.py:126
  153.4 11.5 %select_bitcast_fusion = bf16[64,16384]{0,1:T(8,128)(2,1)} fusion(bf16[16384,64]{1,0:T(8,128)(2,1)} %gather_fusion, pred[16384]{0:T(1024)(128)(4,1)S(1)} %compare_and_fusion.1), kind=kLoop, calls=%fused_computation.62 | loop fusion | flops 1048576 | bytes 4210688 | tf_op jit(solution)/shard_map/jit(_take)/select_n | solution.py:126
  164.9 4.8 copy.54
  169.8 9.2 %multiply_convert_fusion = (bf16[64,16384]{1,0:T(8,128)(2,1)S(1)}, f32[64,16384]{1,0:T(8,128)}) fusion(f32[64]{0:T(128)S(1)} %convert_element_type.121, bf16[192,64]{0,1:T(8,128)(2,1)S(1)} %copy-done, bf16[64,16384]{0,1:T(8,128)(2,1)} %bitcast.132, bf16[64,16384]{0,1:T(8,128)(2,1)} %select_bitcast_fusion, bf16[64,16384]{0,1:T(8,128)(2,1)} %copy.55), kind=kOutput, calls=%fused_computation.66 | convolution fusion | flops 427819008 | bytes 12607744 | tf_op jit(solution)/shard_map/dot_general | solution.py:12
  183.8 7.3 %all-to-all-start.1 = ((bf16[64,16,1024]{2,0,1:T(8,128)(2,1)}), bf16[64,16,1024]{2,0,1:T(8,128)(2,1)S(1)}, u32[]{:S(2)}, u32[]{:S(2)}) async-start(bf16[64,16,1024]{2,0,1:T(8,128)(2,1)} %bitcast.130), calls=%async_computation.1 | async-start | bytes 4194304 | tf_op jit(solution)/shard_map/all_to_all | solution.py:135
  196.4 37.4 %all-to-all-done.1 = bf16[64,16,1024]{2,0,1:T(8,128)(2,1)S(1)} async-done(((bf16[64,16,1024]{2,0,1:T(8,128)(2,1)}), bf16[64,16,1024]{2,0,1:T(8,128)(2,1)S(1)}, u32[]{:S(2)}, u32[]{:S(2)}) %all-to-all-start.1) | async-done | bytes 2097184 | tf_op jit(solution)/shard_map/all_to_all | solution.py:135
  235.4 69.1 %while.42 = (s32[]{:T(128)}, f32[64,4096]{1,0:T(8,128)S(1)}, bf16[64,16384]{1,0:T(8,128)(2,1)}, s32[16384]{0:T(1024)}, s32[]{:T(128)}, /*index=5*/s32[]{:T(128)}, s32[]{:T(128)}, s32[]{:T(128)}) while((s32[]{:T(128)}, f32[64,4096]{1,0:T(8,128)S(1)}, bf16[64,16384]{1,0:T(8,128)(2,1)}, s32[16384]{0:T(1024)}, s32[]{:T(128)}, ...), condition=%wide.region_3.5_spmd.clone, body=%wide.region_2.4_spmd.clone.sunk | while | flops 1082654720 | bytes 2384029 | solution.py:70
  236.1 7.9 %fusion.108 = f32[64,4096]{1,0:T(8,128)S(1)} fusion(s32[2048]{0:T(1024)S(1)} %dynamic_slice.61, f32[64,4096]{1,0:T(8,128)S(1)} %get-tuple-element.504, pred[]{:T(512)S(6)} %compare.10, bf16[64,16384]{1,0:T(8,128)(2,1)} %get-tuple-element.513, s32[]{:T(128)S(6)} %select_n.89), kind=kOutput, calls=%fused_computation.9.clone.1 | convolution fusion | flops 1082654720 | bytes 2367493 | tf_op jit(solution)/shard_map/while/body/eval_jaxpr/dot_general | solution.py:68
  244.8 7.9 %fusion.108 = f32[64,4096]{1,0:T(8,128)S(1)} fusion(s32[2048]{0:T(1024)S(1)} %dynamic_slice.61, f32[64,4096]{1,0:T(8,128)S(1)} %get-tuple-element.504, pred[]{:T(512)S(6)} %compare.10, bf16[64,16384]{1,0:T(8,128)(2,1)} %get-tuple-element.513, s32[]{:T(128)S(6)} %select_n.89), kind=kOutput, calls=%fused_computation.9.clone.1 | convolution fusion | flops 1082654720 | bytes 2367493 | tf_op jit(solution)/shard_map/while/body/eval_jaxpr/dot_general | solution.py:68
  253.4 7.9 %fusion.108 = f32[64,4096]{1,0:T(8,128)S(1)} fusion(s32[2048]{0:T(1024)S(1)} %dynamic_slice.61, f32[64,4096]{1,0:T(8,128)S(1)} %get-tuple-element.504, pred[]{:T(512)S(6)} %compare.10, bf16[64,16384]{1,0:T(8,128)(2,1)} %get-tuple-element.513, s32[]{:T(128)S(6)} %select_n.89), kind=kOutput, calls=%fused_computation.9.clone.1 | convolution fusion | flops 1082654720 | bytes 2367493 | tf_op jit(solution)/shard_map/while/body/eval_jaxpr/dot_general | solution.py:68
  262.0 7.9 %fusion.108 = f32[64,4096]{1,0:T(8,128)S(1)} fusion(s32[2048]{0:T(1024)S(1)} %dynamic_slice.61, f32[64,4096]{1,0:T(8,128)S(1)} %get-tuple-element.504, pred[]{:T(512)S(6)} %compare.10, bf16[64,16384]{1,0:T(8,128)(2,1)} %get-tuple-element.513, s32[]{:T(128)S(6)} %select_n.89), kind=kOutput, calls=%fused_computation.9.clone.1 | convolution fusion | flops 1082654720 | bytes 2367493 | tf_op jit(solution)/shard_map/while/body/eval_jaxpr/dot_general | solution.py:68
  270.7 7.9 %fusion.108 = f32[64,4096]{1,0:T(8,128)S(1)} fusion(s32[2048]{0:T(1024)S(1)} %dynamic_slice.61, f32[64,4096]{1,0:T(8,128)S(1)} %get-tuple-element.504, pred[]{:T(512)S(6)} %compare.10, bf16[64,16384]{1,0:T(8,128)(2,1)} %get-tuple-element.513, s32[]{:T(128)S(6)} %select_n.89), kind=kOutput, calls=%fused_computation.9.clone.1 | convolution fusion | flops 1082654720 | bytes 2367493 | tf_op jit(solution)/shard_map/while/body/eval_jaxpr/dot_general | solution.py:68
  279.3 7.9 %fusion.108 = f32[64,4096]{1,0:T(8,128)S(1)} fusion(s32[2048]{0:T(1024)S(1)} %dynamic_slice.61, f32[64,4096]{1,0:T(8,128)S(1)} %get-tuple-element.504, pred[]{:T(512)S(6)} %compare.10, bf16[64,16384]{1,0:T(8,128)(2,1)} %get-tuple-element.513, s32[]{:T(128)S(6)} %select_n.89), kind=kOutput, calls=%fused_computation.9.clone.1 | convolution fusion | flops 1082654720 | bytes 2367493 | tf_op jit(solution)/shard_map/while/body/eval_jaxpr/dot_general | solution.py:68
  287.9 7.9 %fusion.108 = f32[64,4096]{1,0:T(8,128)S(1)} fusion(s32[2048]{0:T(1024)S(1)} %dynamic_slice.61, f32[64,4096]{1,0:T(8,128)S(1)} %get-tuple-element.504, pred[]{:T(512)S(6)} %compare.10, bf16[64,16384]{1,0:T(8,128)(2,1)} %get-tuple-element.513, s32[]{:T(128)S(6)} %select_n.89), kind=kOutput, calls=%fused_computation.9.clone.1 | convolution fusion | flops 1082654720 | bytes 2367493 | tf_op jit(solution)/shard_map/while/body/eval_jaxpr/dot_general | solution.py:68
  296.5 7.9 %fusion.108 = f32[64,4096]{1,0:T(8,128)S(1)} fusion(s32[2048]{0:T(1024)S(1)} %dynamic_slice.61, f32[64,4096]{1,0:T(8,128)S(1)} %get-tuple-element.504, pred[]{:T(512)S(6)} %compare.10, bf16[64,16384]{1,0:T(8,128)(2,1)} %get-tuple-element.513, s32[]{:T(128)S(6)} %select_n.89), kind=kOutput, calls=%fused_computation.9.clone.1 | convolution fusion | flops 1082654720 | bytes 2367493 | tf_op jit(solution)/shard_map/while/body/eval_jaxpr/dot_general | solution.py:68
  313.7 57.4 %gather_fusion.2 = bf16[16384,64]{1,0:T(8,128)(2,1)} fusion(bf16[64,4096]{0,1:T(8,128)(2,1)S(1)} %copy.58, s32[16384]{0:T(1024)S(1)} %fusion.65), kind=kCustom, calls=%fused_computation.2.clone | custom fusion | bytes 4259840 | tf_op jit(solution)/shard_map/jit(_take)/gather | solution.py:156
  371.1 11.5 %broadcast_select_fusion = bf16[16384,64]{1,0:T(8,128)(2,1)} fusion(bf16[16384,64]{1,0:T(8,128)(2,1)} %gather_fusion.2, pred[16384]{0:T(1024)(128)(4,1)S(1)} %compare_and_fusion), kind=kLoop, calls=%fused_computation.68 | loop fusion | flops 1048576 | bytes 4210688 | tf_op jit(solution)/shard_map/jit(_take)/select_n | solution.py:156
  382.6 4.8 copy.59
  387.4 10.0 %all-to-all-start.2 = ((bf16[64,16,1024]{2,0,1:T(8,128)(2,1)}), bf16[64,16,1024]{2,0,1:T(8,128)(2,1)S(1)}, u32[]{:S(2)}, u32[]{:S(2)}) async-start(bf16[64,16,1024]{2,0,1:T(8,128)(2,1)} %copy.59), calls=%async_computation.2 | async-start | bytes 4194304 | tf_op jit(solution)/shard_map/all_to_all | solution.py:159
  402.1 37.7 %all-to-all-done.2 = bf16[64,16,1024]{2,0,1:T(8,128)(2,1)S(1)} async-done(((bf16[64,16,1024]{2,0,1:T(8,128)(2,1)}), bf16[64,16,1024]{2,0,1:T(8,128)(2,1)S(1)}, u32[]{:S(2)}, u32[]{:S(2)}) %all-to-all-start.2) | async-done | bytes 2097184 | tf_op jit(solution)/shard_map/all_to_all | solution.py:159
  455.8 4.9 fusion.42
  460.7 6.3 fusion.78
  468.9 71.7 %while.43 = (s32[]{:T(128)}, f32[64,4096]{1,0:T(8,128)}, bf16[64,16384]{1,0:T(8,128)(2,1)S(1)}, s32[16384]{0:T(1024)S(1)}, s32[]{:T(128)}, /*index=5*/s32[]{:T(128)}, s32[]{:T(128)}, s32[]{:T(128)}) while((s32[]{:T(128)}, f32[64,4096]{1,0:T(8,128)}, bf16[64,16384]{1,0:T(8,128)(2,1)S(1)}, s32[16384]{0:T(1024)S(1)}, s32[]{:T(128)}, ...), condition=%wide.region_11.13_spmd.clone, body=%wide.region_10.12_spmd.clone.sunk | while | flops 1082654720 | bytes 2384029 | solution.py:70
  468.9 7.9 %fusion.110 = f32[64,4096]{1,0:T(8,128)} fusion(s32[2048]{0:T(1024)S(1)} %dynamic_slice.63, f32[64,4096]{1,0:T(8,128)} %get-tuple-element.552, pred[]{:T(512)S(6)} %compare.11, bf16[64,16384]{1,0:T(8,128)(2,1)S(1)} %get-tuple-element.561, s32[]{:T(128)S(6)} %select_n.90), kind=kOutput, calls=%fused_computation.15.clone.1 | convolution fusion | flops 1082654720 | bytes 2367493 | tf_op jit(solution)/shard_map/while/body/eval_jaxpr/dot_general | solution.py:68
  476.8 9.1 %fusion.110 = f32[64,4096]{1,0:T(8,128)} fusion(s32[2048]{0:T(1024)S(1)} %dynamic_slice.63, f32[64,4096]{1,0:T(8,128)} %get-tuple-element.552, pred[]{:T(512)S(6)} %compare.11, bf16[64,16384]{1,0:T(8,128)(2,1)S(1)} %get-tuple-element.561, s32[]{:T(128)S(6)} %select_n.90), kind=kOutput, calls=%fused_computation.15.clone.1 | convolution fusion | flops 1082654720 | bytes 2367493 | tf_op jit(solution)/shard_map/while/body/eval_jaxpr/dot_general | solution.py:68
  485.9 9.1 %fusion.110 = f32[64,4096]{1,0:T(8,128)} fusion(s32[2048]{0:T(1024)S(1)} %dynamic_slice.63, f32[64,4096]{1,0:T(8,128)} %get-tuple-element.552, pred[]{:T(512)S(6)} %compare.11, bf16[64,16384]{1,0:T(8,128)(2,1)S(1)} %get-tuple-element.561, s32[]{:T(128)S(6)} %select_n.90), kind=kOutput, calls=%fused_computation.15.clone.1 | convolution fusion | flops 1082654720 | bytes 2367493 | tf_op jit(solution)/shard_map/while/body/eval_jaxpr/dot_general | solution.py:68
  495.0 9.1 %fusion.110 = f32[64,4096]{1,0:T(8,128)} fusion(s32[2048]{0:T(1024)S(1)} %dynamic_slice.63, f32[64,4096]{1,0:T(8,128)} %get-tuple-element.552, pred[]{:T(512)S(6)} %compare.11, bf16[64,16384]{1,0:T(8,128)(2,1)S(1)} %get-tuple-element.561, s32[]{:T(128)S(6)} %select_n.90), kind=kOutput, calls=%fused_computation.15.clone.1 | convolution fusion | flops 1082654720 | bytes 2367493 | tf_op jit(solution)/shard_map/while/body/eval_jaxpr/dot_general | solution.py:68
  504.1 9.1 %fusion.110 = f32[64,4096]{1,0:T(8,128)} fusion(s32[2048]{0:T(1024)S(1)} %dynamic_slice.63, f32[64,4096]{1,0:T(8,128)} %get-tuple-element.552, pred[]{:T(512)S(6)} %compare.11, bf16[64,16384]{1,0:T(8,128)(2,1)S(1)} %get-tuple-element.561, s32[]{:T(128)S(6)} %select_n.90), kind=kOutput, calls=%fused_computation.15.clone.1 | convolution fusion | flops 1082654720 | bytes 2367493 | tf_op jit(solution)/shard_map/while/body/eval_jaxpr/dot_general | solution.py:68
  513.2 9.1 %fusion.110 = f32[64,4096]{1,0:T(8,128)} fusion(s32[2048]{0:T(1024)S(1)} %dynamic_slice.63, f32[64,4096]{1,0:T(8,128)} %get-tuple-element.552, pred[]{:T(512)S(6)} %compare.11, bf16[64,16384]{1,0:T(8,128)(2,1)S(1)} %get-tuple-element.561, s32[]{:T(128)S(6)} %select_n.90), kind=kOutput, calls=%fused_computation.15.clone.1 | convolution fusion | flops 1082654720 | bytes 2367493 | tf_op jit(solution)/shard_map/while/body/eval_jaxpr/dot_general | solution.py:68
  522.3 9.1 %fusion.110 = f32[64,4096]{1,0:T(8,128)} fusion(s32[2048]{0:T(1024)S(1)} %dynamic_slice.63, f32[64,4096]{1,0:T(8,128)} %get-tuple-element.552, pred[]{:T(512)S(6)} %compare.11, bf16[64,16384]{1,0:T(8,128)(2,1)S(1)} %get-tuple-element.561, s32[]{:T(128)S(6)} %select_n.90), kind=kOutput, calls=%fused_computation.15.clone.1 | convolution fusion | flops 1082654720 | bytes 2367493 | tf_op jit(solution)/shard_map/while/body/eval_jaxpr/dot_general | solution.py:68
  531.4 9.1 %fusion.110 = f32[64,4096]{1,0:T(8,128)} fusion(s32[2048]{0:T(1024)S(1)} %dynamic_slice.63, f32[64,4096]{1,0:T(8,128)} %get-tuple-element.552, pred[]{:T(512)S(6)} %compare.11, bf16[64,16384]{1,0:T(8,128)(2,1)S(1)} %get-tuple-element.561, s32[]{:T(128)S(6)} %select_n.90), kind=kOutput, calls=%fused_computation.15.clone.1 | convolution fusion | flops 1082654720 | bytes 2367493 | tf_op jit(solution)/shard_map/while/body/eval_jaxpr/dot_general | solution.py:68
  540.5 9.9 %all-to-all-start.3 = ((bf16[64,16,1024]{2,0,1:T(8,128)(2,1)}), bf16[64,16,1024]{2,0,1:T(8,128)(2,1)}, u32[]{:S(2)}, u32[]{:S(2)}) async-start(bf16[64,16,1024]{2,0,1:T(8,128)(2,1)} %bitcast.128), calls=%async_computation.3 | async-start | bytes 4194304 | tf_op jit(solution)/shard_map/all_to_all | solution.py:171
  553.5 5.2 fusion.32
  558.7 35.8 %all-to-all-done.3 = bf16[64,16,1024]{2,0,1:T(8,128)(2,1)} async-done(((bf16[64,16,1024]{2,0,1:T(8,128)(2,1)}), bf16[64,16,1024]{2,0,1:T(8,128)(2,1)}, u32[]{:S(2)}, u32[]{:S(2)}) %all-to-all-start.3) | async-done | bytes 2097184 | tf_op jit(solution)/shard_map/all_to_all | solution.py:171
  597.6 79.9 %while.44 = (s32[]{:T(128)}, f32[64,4096]{1,0:T(8,128)}, bf16[64,16384]{1,0:T(8,128)(2,1)}, s32[16384]{0:T(1024)}, s32[]{:T(128)}, /*index=5*/s32[]{:T(128)}, s32[]{:T(128)}, s32[]{:T(128)}) while((s32[]{:T(128)}, f32[64,4096]{1,0:T(8,128)}, bf16[64,16384]{1,0:T(8,128)(2,1)}, s32[16384]{0:T(1024)}, s32[]{:T(128)}, ...), condition=%wide.region_13.15_spmd.clone, body=%wide.region_12.14_spmd.clone.sunk | while | flops 1082654720 | bytes 2384029 | solution.py:70
  598.7 8.9 %fusion.112 = f32[64,4096]{1,0:T(8,128)} fusion(s32[2048]{0:T(1024)S(1)} %dynamic_slice.65, f32[64,4096]{1,0:T(8,128)} %get-tuple-element.528, pred[]{:T(512)S(6)} %compare.12, bf16[64,16384]{1,0:T(8,128)(2,1)} %get-tuple-element.537, s32[]{:T(128)S(6)} %select_n.91), kind=kOutput, calls=%fused_computation.21.clone.1 | convolution fusion | flops 1082654720 | bytes 2367493 | tf_op jit(solution)/shard_map/while/body/eval_jaxpr/dot_general | solution.py:68
  608.3 9.3 %fusion.112 = f32[64,4096]{1,0:T(8,128)} fusion(s32[2048]{0:T(1024)S(1)} %dynamic_slice.65, f32[64,4096]{1,0:T(8,128)} %get-tuple-element.528, pred[]{:T(512)S(6)} %compare.12, bf16[64,16384]{1,0:T(8,128)(2,1)} %get-tuple-element.537, s32[]{:T(128)S(6)} %select_n.91), kind=kOutput, calls=%fused_computation.21.clone.1 | convolution fusion | flops 1082654720 | bytes 2367493 | tf_op jit(solution)/shard_map/while/body/eval_jaxpr/dot_general | solution.py:68
  618.3 9.3 %fusion.112 = f32[64,4096]{1,0:T(8,128)} fusion(s32[2048]{0:T(1024)S(1)} %dynamic_slice.65, f32[64,4096]{1,0:T(8,128)} %get-tuple-element.528, pred[]{:T(512)S(6)} %compare.12, bf16[64,16384]{1,0:T(8,128)(2,1)} %get-tuple-element.537, s32[]{:T(128)S(6)} %select_n.91), kind=kOutput, calls=%fused_computation.21.clone.1 | convolution fusion | flops 1082654720 | bytes 2367493 | tf_op jit(solution)/shard_map/while/body/eval_jaxpr/dot_general | solution.py:68
  628.3 9.3 %fusion.112 = f32[64,4096]{1,0:T(8,128)} fusion(s32[2048]{0:T(1024)S(1)} %dynamic_slice.65, f32[64,4096]{1,0:T(8,128)} %get-tuple-element.528, pred[]{:T(512)S(6)} %compare.12, bf16[64,16384]{1,0:T(8,128)(2,1)} %get-tuple-element.537, s32[]{:T(128)S(6)} %select_n.91), kind=kOutput, calls=%fused_computation.21.clone.1 | convolution fusion | flops 1082654720 | bytes 2367493 | tf_op jit(solution)/shard_map/while/body/eval_jaxpr/dot_general | solution.py:68
  638.3 9.3 %fusion.112 = f32[64,4096]{1,0:T(8,128)} fusion(s32[2048]{0:T(1024)S(1)} %dynamic_slice.65, f32[64,4096]{1,0:T(8,128)} %get-tuple-element.528, pred[]{:T(512)S(6)} %compare.12, bf16[64,16384]{1,0:T(8,128)(2,1)} %get-tuple-element.537, s32[]{:T(128)S(6)} %select_n.91), kind=kOutput, calls=%fused_computation.21.clone.1 | convolution fusion | flops 1082654720 | bytes 2367493 | tf_op jit(solution)/shard_map/while/body/eval_jaxpr/dot_general | solution.py:68
  648.3 9.3 %fusion.112 = f32[64,4096]{1,0:T(8,128)} fusion(s32[2048]{0:T(1024)S(1)} %dynamic_slice.65, f32[64,4096]{1,0:T(8,128)} %get-tuple-element.528, pred[]{:T(512)S(6)} %compare.12, bf16[64,16384]{1,0:T(8,128)(2,1)} %get-tuple-element.537, s32[]{:T(128)S(6)} %select_n.91), kind=kOutput, calls=%fused_computation.21.clone.1 | convolution fusion | flops 1082654720 | bytes 2367493 | tf_op jit(solution)/shard_map/while/body/eval_jaxpr/dot_general | solution.py:68
  658.3 9.3 %fusion.112 = f32[64,4096]{1,0:T(8,128)} fusion(s32[2048]{0:T(1024)S(1)} %dynamic_slice.65, f32[64,4096]{1,0:T(8,128)} %get-tuple-element.528, pred[]{:T(512)S(6)} %compare.12, bf16[64,16384]{1,0:T(8,128)(2,1)} %get-tuple-element.537, s32[]{:T(128)S(6)} %select_n.91), kind=kOutput, calls=%fused_computation.21.clone.1 | convolution fusion | flops 1082654720 | bytes 2367493 | tf_op jit(solution)/shard_map/while/body/eval_jaxpr/dot_general | solution.py:68
  668.2 9.3 %fusion.112 = f32[64,4096]{1,0:T(8,128)} fusion(s32[2048]{0:T(1024)S(1)} %dynamic_slice.65, f32[64,4096]{1,0:T(8,128)} %get-tuple-element.528, pred[]{:T(512)S(6)} %compare.12, bf16[64,16384]{1,0:T(8,128)(2,1)} %get-tuple-element.537, s32[]{:T(128)S(6)} %select_n.91), kind=kOutput, calls=%fused_computation.21.clone.1 | convolution fusion | flops 1082654720 | bytes 2367493 | tf_op jit(solution)/shard_map/while/body/eval_jaxpr/dot_general | solution.py:68
  680.1 19.6 %all-reduce.3.cloned.1.call-done = (f32[192,64]{0,1:T(8,128)}, f32[64]{0:T(128)}, f32[64,64]{1,0:T(8,128)}, f32[64]{0:T(128)}, f32[64]{0:T(128)}, /*index=5*/f32...) async-done(((f32[192,64]{0,1:T(8,128)}, f32[64]{0:T(128)}, f32[64,64]{1,0:T(8,128)}, ...) | async-done | bytes 116752 | tf_op jit(solution)/shard_map/psum | solution.py:184
  (177 shorter events, 84.4 us)
Async XLA Ops:
  7.2 162.6 %copy-start = (bf16[192,64]{0,1:T(8,128)(2,1)S(1)}, bf16[192,64]{0,1:T(8,128)(2,1)}, u32[]{:S(2)}) copy-start(bf16[192,64]{0,1:T(8,128)(2,1)} %param.38) | copy-start | bytes 73732
  79.3 13.2 %copy-start.26 = (s32[16]{0:T(128)S(1)}, s32[16]{0:T(128)}, u32[]{:S(2)}) copy-start(s32[16]{0:T(128)} %param.34) | copy-start | bytes 196
  79.3 13.4 %copy-start.18 = (s32[16384]{0:T(1024)S(1)}, s32[16384]{0:T(1024)}, u32[]{:S(2)}) copy-start(s32[16384]{0:T(1024)} %param.32) | copy-start | bytes 196612
  79.3 13.4 %copy-start.34 = (bf16[64]{0:T(256)(128)(2,1)S(1)}, bf16[64]{0:T(256)(128)(2,1)}, u32[]{:S(2)}) copy-start(bf16[64]{0:T(256)(128)(2,1)} %param.42) | copy-start | bytes 388
  79.3 13.4 %copy-start.35 = (bf16[64]{0:T(256)(128)(2,1)S(1)}, bf16[64]{0:T(256)(128)(2,1)}, u32[]{:S(2)}) copy-start(bf16[64]{0:T(256)(128)(2,1)} %param.39) | copy-start | bytes 388
  79.4 13.5 %copy-start.36 = (bf16[64]{0:T(256)(128)(2,1)S(1)}, bf16[64]{0:T(256)(128)(2,1)}, u32[]{:S(2)}) copy-start(bf16[64]{0:T(256)(128)(2,1)} %param.41) | copy-start | bytes 388
  79.4 13.5 %copy-start.37 = (bf16[64]{0:T(256)(128)(2,1)S(1)}, bf16[64]{0:T(256)(128)(2,1)}, u32[]{:S(2)}) copy-start(bf16[64]{0:T(256)(128)(2,1)} %param.43) | copy-start | bytes 388
  84.2 80.7 %all-to-all-start = ((bf16[64,16,1024]{2,0,1:T(8,128)(2,1)}), bf16[64,16,1024]{2,0,1:T(8,128)(2,1)}, u32[]{:S(2)}, u32[]{:S(2)}) async-start(bf16[64,16,1024]{2,0,1:T(8,128)(2,1)} %copy.53), calls=%async_computation | async-start | bytes 4194304 | tf_op jit(solution)/shard_map/all_to_all | solution.py:128
  92.8 88.1 %copy-start.24 = (f32[64]{0:T(128)}, f32[64]{0:T(128)S(1)}, u32[]{:S(2)}) copy-start(f32[64]{0:T(128)S(1)} %convert_element_type.124) | copy-start | bytes 772
  92.9 57.4 %copy-start.6 = (bf16[64,16384]{1,0:T(8,128)(2,1)S(1)}, bf16[64,16384]{1,0:T(8,128)(2,1)}, u32[]{:S(2)}) copy-start(bf16[64,16384]{1,0:T(8,128)(2,1)} %param.30) | copy-start | bytes 6291460
  169.8 9.2 %copy-start.21 = (bf16[64,64]{1,0:T(8,128)(2,1)S(1)}, bf16[64,64]{1,0:T(8,128)(2,1)}, u32[]{:S(2)}) copy-start(bf16[64,64]{1,0:T(8,128)(2,1)} %param.40) | copy-start | bytes 24580
  179.0 1.3 copy-start.4
  180.3 1.9 copy-start.1
  182.3 13.5 %copy-start.22 = (s32[4096]{0:T(1024)S(1)}, s32[4096]{0:T(1024)}, u32[]{:S(2)}) copy-start(s32[4096]{0:T(1024)} %param.36) | copy-start | bytes 49156
  183.8 50.0 %all-to-all-start.1 = ((bf16[64,16,1024]{2,0,1:T(8,128)(2,1)}), bf16[64,16,1024]{2,0,1:T(8,128)(2,1)S(1)}, u32[]{:S(2)}, u32[]{:S(2)}) async-start(bf16[64,16,1024]{2,0,1:T(8,128)(2,1)} %bitcast.130), calls=%async_computation.1 | async-start | bytes 4194304 | tf_op jit(solution)/shard_map/all_to_all | solution.py:135
  235.4 69.2 %copy-start.13 = (bf16[64,4096]{1,0:T(8,128)(2,1)S(1)}, bf16[64,4096]{1,0:T(8,128)(2,1)}, u32[]{:S(2)}) copy-start(bf16[64,4096]{1,0:T(8,128)(2,1)} %param.29) | copy-start | bytes 1572868
  235.4 69.2 %copy-start.20 = (bf16[128,64]{0,1:T(8,128)(2,1)S(1)}, bf16[128,64]{0,1:T(8,128)(2,1)}, u32[]{:S(2)}) copy-start(bf16[128,64]{0,1:T(8,128)(2,1)} %param.44) | copy-start | bytes 49156
  235.4 69.2 %copy-start.38 = (f32[64]{0:T(128)S(1)}, f32[64]{0:T(128)}, u32[]{:S(2)}) copy-start(f32[64]{0:T(128)} %convert_element_type.129) | copy-start | bytes 772
  304.5 0.7 copy-start.19
  304.5 0.7 copy-start.30
  304.6 1.1 copy-start.16
  304.6 1.4 copy-start.23
  304.6 1.4 copy-start.28
  304.6 1.3 copy-start.29
  304.6 1.3 copy-start.31
  304.6 1.3 copy-start.32
  304.6 1.3 copy-start.33
  305.1 0.8 copy-start.14
  309.4 2.4 copy-start.15
  310.5 0.8 copy-start.17
  311.8 1.4 copy-start.8
  382.6 14.8 %copy-start.27 = (s32[16]{0:T(128)S(1)}, s32[16]{0:T(128)}, u32[]{:S(2)}) copy-start(s32[16]{0:T(128)} %param.34) | copy-start | bytes 196
  387.4 52.4 %copy-start.25 = (f32[64]{0:T(128)S(1)}, f32[64]{0:T(128)}, u32[]{:S(2)}) copy-start(f32[64]{0:T(128)} %copy-done.24) | copy-start | bytes 772
  387.4 52.4 %all-to-all-start.2 = ((bf16[64,16,1024]{2,0,1:T(8,128)(2,1)}), bf16[64,16,1024]{2,0,1:T(8,128)(2,1)S(1)}, u32[]{:S(2)}, u32[]{:S(2)}) async-start(bf16[64,16,1024]{2,0,1:T(8,128)(2,1)} %copy.59), calls=%async_computation.2 | async-start | bytes 4194304 | tf_op jit(solution)/shard_map/all_to_all | solution.py:159
  441.8 3.7 copy-start.2
  442.1 5.7 copy-start.3
  447.8 2.6 copy-start.39
  450.4 2.7 copy-start.7
  450.4 2.9 copy-start.10
  450.4 4.2 copy-start.11
  450.4 5.4 copy-start.12
  540.5 10.0 %copy-start.5 = (bf16[64,16384]{1,0:T(8,128)(2,1)S(1)}, bf16[64,16384]{1,0:T(8,128)(2,1)}, u32[]{:S(2)}) copy-start(bf16[64,16384]{1,0:T(8,128)(2,1)} %copy-done.4) | copy-start | bytes 6291460
  540.5 53.9 %all-to-all-start.3 = ((bf16[64,16,1024]{2,0,1:T(8,128)(2,1)}), bf16[64,16,1024]{2,0,1:T(8,128)(2,1)}, u32[]{:S(2)}, u32[]{:S(2)}) async-start(bf16[64,16,1024]{2,0,1:T(8,128)(2,1)} %bitcast.128), calls=%async_computation.3 | async-start | bytes 4194304 | tf_op jit(solution)/shard_map/all_to_all | solution.py:171
  550.5 149.2 %all-reduce.3.cloned.1.call-start = ((), (), s32[]{:S(2)}) async-start(), calls=%async_computation.4 | async-start | bytes 335872 | tf_op jit(solution)/shard_map/psum | solution.py:184
  597.6 79.9 %copy-start.9 = (f32[128,4096]{1,0:T(8,128)S(1)}, f32[128,4096]{1,0:T(8,128)}, u32[]{:S(2)}) copy-start(f32[128,4096]{1,0:T(8,128)} %copy-done.8) | copy-start | bytes 6291460
Sparse Core Ops, SparseCore 0:
  558.9 140.7 all-reduce.2
where the time goes:
time: 732 us; the launch traced here: 722 us
  matrix products  244 us (33%)
  local copies, waits for them, and re-layouts  236 us (32%)
  waiting for transfers between devices  131 us (18%)
  other arithmetic  60 us (8%)
  starting transfers between devices  35.7 us (5%)
  between operations  15.1 us (2%)
    dot_general x24, matrix products, advance(): jnp.dot(piece_cols, one_hot, preferred_element_type=jnp.float32)  209 us
    gather x1, local copies, waits for them, and re-layouts, per_device(): jnp.take(aggregate_grad, receivers, axis=1)  57.4 us
    gather x1, local copies, waits for them, and re-layouts, per_device(): owner_rows = jnp.take(nodes, receivers, axis=1)  57.4 us
    gather x1, local copies, waits for them, and re-layouts, per_device(): sender_cols = jnp.take(nodes, senders, axis=1)  57.4 us
    all_to_all x1, waiting for transfers between devices, per_device(): lax.all_to_all(owner_grad, 'edge', split_axis=1, concat_axis=1, tiled=True)  37.7 us
    all_to_all x1, waiting for transfers between devices, per_device(): lax.all_to_all(message, 'edge', split_axis=1, concat_axis=1, tiled=True)  37.4 us
    all_to_all x1, waiting for transfers between devices, per_device(): lax.all_to_all(receiver_grad, 'edge', split_axis=1, concat_axis=1, tiled=...  35.8 us
    unnamed x97, local copies, waits for them, and re-layouts  28.9 us
  transfers between devices with their start and end apart: 5, of which 4 were waited for; matrix products, arithmetic and copies ran while one was open for 24% of the time, Pallas kernels for 0%

commit v1 on v0

v1 whole, which is shorter than its diff:
```python
import functools

import jax
import jax.numpy as jnp
from jax import lax
from jax.experimental import pallas as pl
from jax.experimental.pallas import tpu as pltpu
from jax.sharding import PartitionSpec as P

NORM_EPS = 1e-05
F32 = jnp.float32
BF16 = jnp.bfloat16
LOW = 256
VMEM_LIMIT = 56 * 2**20

EB1, EB2, EG, EH, NB1, NB2, NG, NH, CM = 0, 1, 2, 3, 4, 5, 6, 7, 8


def dot(a, b):
    return jnp.dot(a, b, preferred_element_type=F32)


def dot_tn(a, b):
    return lax.dot_general(a, b, (((0,), (0,)), ((), ())), preferred_element_type=F32)


def dot_nt(a, b):
    return lax.dot_general(a, b, (((1,), (1,)), ((), ())), preferred_element_type=F32)


def one_hot_low(ids):
    low = ids & (LOW - 1)
    rows = lax.broadcasted_iota(jnp.int32, (LOW, ids.shape[1]), 0)
    return (rows == low).astype(F32).astype(BF16)


def high_of(ids, rows):
    high = ids >> (LOW.bit_length() - 1)
    return jnp.broadcast_to(high.astype(F32).astype(BF16), (rows, ids.shape[1]))


def stack_table(table_ref, value):
    rows = value.shape[0]
    for h in range(value.shape[1] // LOW):
        table_ref[h * rows : (h + 1) * rows, :] = value[:, h * LOW : (h + 1) * LOW]


def gather_columns(table, ids, rows):
    picked = dot(table, one_hot_low(ids)).astype(BF16)
    high = high_of(ids, rows)
    out = picked[:rows]
    for h in range(1, table.shape[0] // rows):
        out = jnp.where(high == BF16(h), picked[h * rows : (h + 1) * rows], out)
    return out


def scatter_columns(values, ids, count):
    rows = values.shape[0]
    high = high_of(ids, rows)
    zero = jnp.zeros_like(values)
    spread = jnp.concatenate(
        [jnp.where(high == BF16(h), values, zero) for h in range(count // LOW)], axis=0
    )
    return dot_nt(spread, one_hot_low(ids))


def unstack(table):
    rows = 64
    return jnp.concatenate(
        [table[h * rows : (h + 1) * rows] for h in range(table.shape[0] // rows)], axis=1
    )


def column(cols, index):
    return cols[:, index : index + 1]


def mean_rows(v):
    return jnp.mean(v, axis=0, keepdims=True)


def lane_sums(v):
    out = v[:, :128]
    for k in range(1, v.shape[1] // 128):
        out = out + v[:, k * 128 : (k + 1) * 128]
    return out


def branch_forward(w1, w2, b1, b2, stacked):
    pre = dot_tn(w1, stacked) + b1
    hidden = (pre * (1.0 / (1.0 + jnp.exp(-pre)))).astype(BF16)
    outer = dot_tn(w2, hidden) + b2
    shifted = outer - mean_rows(outer)
    inverse = lax.rsqrt(mean_rows(shifted * shifted) + NORM_EPS)
    return pre, hidden, shifted * inverse, inverse


def branch_backward(w2, gain, grad, pre, normal, inverse):
    q = grad * gain
    outer_grad = (
        inverse * (q - mean_rows(q) - normal * mean_rows(q * normal))
    ).astype(BF16)
    s = 1.0 / (1.0 + jnp.exp(-pre))
    pre_grad = (dot(w2, outer_grad) * (s * (1.0 + pre * (1.0 - s)))).astype(BF16)
    return outer_grad, pre_grad


def gather_kernel(cap, table_ref, ids_ref, out_ref, stacked):
    rows = table_ref.shape[0]

    @pl.when(pl.program_id(0) == 0)
    def _():
        stack_table(stacked, table_ref[...])

    got = gather_columns(stacked[...], ids_ref[...], rows)
    for k in range(out_ref.shape[0]):
        out_ref[k] = got[:, k * cap : (k + 1) * cap]


def gather_for_owners(table, ids, owners, step):
    rows, count = table.shape
    slots = ids.shape[1]
    cap = slots // owners
    return pl.pallas_call(
        functools.partial(gather_kernel, cap),
        grid=(slots // step,),
        in_specs=[
            pl.BlockSpec((rows, count), lambda i: (0, 0)),
            pl.BlockSpec((1, step), lambda i: (0, i)),
        ],
        out_specs=pl.BlockSpec((step // cap, rows, cap), lambda i: (i, 0, 0)),
        out_shape=jax.ShapeDtypeStruct((owners, rows, cap), BF16),
        scratch_shapes=[pltpu.VMEM((rows * (count // LOW), LOW), BF16)],
        compiler_params=pltpu.CompilerParams(vmem_limit_bytes=VMEM_LIMIT),
        name="gather_columns",
    )(table, ids)


def live_of(counts_ref, step, cap):
    place = lax.broadcasted_iota(jnp.int32, (1, cap), 1)
    base = pl.program_id(0) * (step // cap)
    return jnp.concatenate(
        [(place < counts_ref[base + k]).astype(F32) for k in range(step // cap)], axis=1
    )


def edge_forward_kernel(
    cap, counts_ref, nodes_ref, edges_ref, got_ref, senders_ref, w1_ref, w2_ref, cols_ref,
    message_ref, pre_ref, normal_ref, inverse_ref, stacked,
):
    rows, step = edges_ref.shape

    @pl.when(pl.program_id(0) == 0)
    def _():
        stack_table(stacked, nodes_ref[...])

    cols = cols_ref[...]
    sent = gather_columns(stacked[...], senders_ref[...], rows)
    got = jnp.concatenate([got_ref[k] for k in range(step // cap)], axis=1)
    edges = edges_ref[...]
    pre, _, normal, inverse = branch_forward(
        w1_ref[...], w2_ref[...], column(cols, EB1), column(cols, EB2),
        jnp.concatenate([edges, sent, got], axis=0),
    )
    pre_ref[...] = pre
    normal_ref[...] = normal
    inverse_ref[...] = inverse
    live = live_of(counts_ref, step, cap)
    message = (
        (edges.astype(F32) + (normal * column(cols, EG) + column(cols, EH))) * live
    ).astype(BF16)
    for k in range(step // cap):
        message_ref[k] = message[:, k * cap : (k + 1) * cap]


def edge_forward(counts, nodes, edges, got, senders, w1, w2, cols, step):
    rows, slots = edges.shape
    owners = got.shape[0]
    cap = slots // owners
    whole = lambda a: pl.BlockSpec(a.shape, lambda i: (0,) * a.ndim)
    wide = pl.BlockSpec((rows, step), lambda i: (0, i))
    split = pl.BlockSpec((step // cap, rows, cap), lambda i: (i, 0, 0))
    line = pl.BlockSpec((1, step), lambda i: (0, i))
    return pl.pallas_call(
        functools.partial(edge_forward_kernel, cap),
        grid=(slots // step,),
        in_specs=[
            pl.BlockSpec(memory_space=pltpu.SMEM), whole(nodes), wide, split, line,
            whole(w1), whole(w2), whole(cols),
        ],
        out_specs=[split, wide, wide, line],
        out_shape=[
            jax.ShapeDtypeStruct((owners, rows, cap), BF16),
            jax.ShapeDtypeStruct((rows, slots), F32),
            jax.ShapeDtypeStruct((rows, slots), F32),
            jax.ShapeDtypeStruct((1, slots), F32),
        ],
        scratch_shapes=[pltpu.VMEM((rows * (nodes.shape[1] // LOW), LOW), BF16)],
        compiler_params=pltpu.CompilerParams(vmem_limit_bytes=VMEM_LIMIT),
        name="edge_forward",
    )(counts, nodes, edges, got, senders, w1, w2, cols)


def node_kernel(
    cap, levels_count, arrived_ref, receivers_ref, nodes_ref, target_ref, levels_ref, land_ref,
    w1_ref, w2_ref, cols_ref,
    new_ref, part_ref, agg_grad_ref, first_ref, second_ref, vec_ref, total,
):
    rows, count = nodes_ref.shape
    step = receivers_ref.shape[1]

    @pl.when(pl.program_id(0) == 0)
    def _():
        total[...] = jnp.zeros_like(total)

    arrived = jnp.concatenate([arrived_ref[k] for k in range(step // cap)], axis=1)
    total[...] += scatter_columns(arrived, receivers_ref[...], count)

    @pl.when(pl.program_id(0) == pl.num_programs(0) - 1)
    def _():
        cols = cols_ref[...]
        aggregate = unstack(total[...]).astype(BF16)
        nodes = nodes_ref[...]
        stacked = jnp.concatenate([nodes, aggregate], axis=0)
        pre, hidden, normal, inverse = branch_forward(
            w1_ref[...], w2_ref[...], column(cols, NB1), column(cols, NB2), stacked
        )
        gain = column(cols, NG)
        state = nodes.astype(F32) + (normal * gain + column(cols, NH))
        new_ref[...] = state.astype(BF16)
        levels = levels_ref[...]
        weight = jnp.zeros((rows, count), F32)
        for l in range(levels_count):
            weight = jnp.where(levels == l, column(cols, CM + l), weight)
        weight = weight * land_ref[...].astype(F32)
        grad = weight * (state - target_ref[...].astype(F32))
        outer_grad, pre_grad = branch_backward(w2_ref[...], gain, grad, pre, normal, inverse)
        stacked_grad = dot(w1_ref[...], pre_grad)
        part_ref[...] = grad + stacked_grad[:rows]
        agg_grad_ref[...] = stacked_grad[rows:].astype(BF16)
        first_ref[...] = dot_nt(stacked, pre_grad)
        second_ref[...] = dot_nt(hidden, outer_grad)
        sums = [
            lane_sums(v).sum(axis=1, keepdims=True)
            for v in (pre_grad.astype(F32), outer_grad.astype(F32), grad * normal, grad)
        ]
        vec_ref[...] = jnp.concatenate(sums, axis=1)


def node_step(arrived, receivers, nodes, target, levels, land, w1, w2, cols, levels_count, step):
    owners, rows, cap = arrived.shape
    count = nodes.shape[1]
    slots = receivers.shape[1]
    whole = lambda a: pl.BlockSpec(a.shape, lambda i: (0,) * len(a.shape))
    outs = [
        jax.ShapeDtypeStruct((rows, count), BF16),
        jax.ShapeDtypeStruct((rows, count), F32),
        jax.ShapeDtypeStruct((rows, count), BF16),
        jax.ShapeDtypeStruct(w1.shape, F32),
        jax.ShapeDtypeStruct(w2.shape, F32),
        jax.ShapeDtypeStruct((rows, 4), F32),
    ]
    return pl.pallas_call(
        functools.partial(node_kernel, cap, levels_count),
        grid=(slots // step,),
        in_specs=[
            pl.BlockSpec((step // cap, rows, cap), lambda i: (i, 0, 0)),
            pl.BlockSpec((1, step), lambda i: (0, i)),
            *(whole(a) for a in (nodes, target, levels, land, w1, w2, cols)),
        ],
        out_specs=[whole(o) for o in outs],
        out_shape=outs,
        scratch_shapes=[pltpu.VMEM((rows * (count // LOW), LOW), F32)],
        compiler_params=pltpu.CompilerParams(vmem_limit_bytes=VMEM_LIMIT),
        name="sum_and_nodes",
    )(arrived, receivers, nodes, target, levels, land, w1, w2, cols)


def edge_backward_kernel(
    cap, count, counts_ref, back_ref, edges_ref, pre_ref, normal_ref, inverse_ref, senders_ref,
    w1_ref, w2_ref, cols_ref,
    edge_grad_ref, pre_grad_ref, sent_ref, pair_ref, vec_ref, sums,
):
    rows, step = edges_ref.shape

    @pl.when(pl.program_id(0) == 0)
    def _():
        sent_ref[...] = jnp.zeros_like(sent_ref)
        pair_ref[...] = jnp.zeros_like(pair_ref)
        sums[...] = jnp.zeros_like(sums)

    cols = cols_ref[...]
    live = live_of(counts_ref, step, cap)
    grad = jnp.concatenate([back_ref[k] for k in range(step // cap)], axis=1).astype(F32) * live
    pre, normal = pre_ref[...], normal_ref[...]
    outer_grad, pre_grad = branch_backward(
        w2_ref[...], column(cols, EG), grad, pre, normal, inverse_ref[...]
    )
    hidden = (pre * (1.0 / (1.0 + jnp.exp(-pre)))).astype(BF16)
    edges = edges_ref[...]
    edge_grad_ref[...] = (grad + dot(w1_ref[:rows, :], pre_grad)).astype(BF16)
    for k in range(step // cap):
        pre_grad_ref[k] = pre_grad[:, k * cap : (k + 1) * cap]
    sent_ref[...] += scatter_columns(pre_grad, senders_ref[...], count)
    pair_ref[...] += dot_nt(
        jnp.concatenate([edges, hidden], axis=0), jnp.concatenate([pre_grad, outer_grad], axis=0)
    )
    for k, v in enumerate((pre_grad.astype(F32), outer_grad.astype(F32), grad * normal, grad)):
        sums[k] += lane_sums(v)

    @pl.when(pl.program_id(0) == pl.num_programs(0) - 1)
    def _():
        vec_ref[...] = jnp.concatenate(
            [sums[k].sum(axis=1, keepdims=True) for k in range(4)], axis=1
        )


def edge_backward(counts, back, edges, pre, normal, inverse, senders, w1, w2, cols, count, step):
    rows, slots = edges.shape
    owners, _, cap = back.shape
    whole = lambda a: pl.BlockSpec(a.shape, lambda i: (0,) * len(a.shape))
    wide = pl.BlockSpec((rows, step), lambda i: (0, i))
    split = pl.BlockSpec((step // cap, rows, cap), lambda i: (i, 0, 0))
    line = pl.BlockSpec((1, step), lambda i: (0, i))
    outs = [
        jax.ShapeDtypeStruct((rows, slots), BF16),
        jax.ShapeDtypeStruct((owners, rows, cap), BF16),
        jax.ShapeDtypeStruct((rows * (count // LOW), LOW), F32),
        jax.ShapeDtypeStruct((2 * rows, 2 * rows), F32),
        jax.ShapeDtypeStruct((rows, 4), F32),
    ]
    return pl.pallas_call(
        functools.partial(edge_backward_kernel, cap, count),
        grid=(slots // step,),
        in_specs=[
            pl.BlockSpec(memory_space=pltpu.SMEM), split, wide, wide, wide, line, line,
            whole(w1), whole(w2), whole(cols),
        ],
        out_specs=[wide, split, *(whole(o) for o in outs[2:])],
        out_shape=outs,
        scratch_shapes=[pltpu.VMEM((4, rows, 128), F32)],
        compiler_params=pltpu.CompilerParams(vmem_limit_bytes=VMEM_LIMIT),
        name="edge_backward",
    )(counts, back, edges, pre, normal, inverse, senders, w1, w2, cols)


def split_dot_nt(low, wide):
    top = wide.astype(BF16)
    rest = (wide - top.astype(F32)).astype(BF16)
    return dot_nt(low, top) + dot_nt(low, rest)


def split_dot(low, wide):
    top = wide.astype(BF16)
    rest = (wide - top.astype(F32)).astype(BF16)
    return dot(low, top) + dot(low, rest)


def finish_kernel(
    cap, returned_ref, receivers_ref, nodes_ref, part_ref, sent_ref, w1_ref,
    out_ref, rest_ref, total,
):
    rows, count = nodes_ref.shape
    step = receivers_ref.shape[1]

    @pl.when(pl.program_id(0) == 0)
    def _():
        total[...] = jnp.zeros_like(total)

    returned = jnp.concatenate([returned_ref[k] for k in range(step // cap)], axis=1)
    total[...] += scatter_columns(returned, receivers_ref[...], count)

    @pl.when(pl.program_id(0) == pl.num_programs(0) - 1)
    def _():
        sent, got = unstack(sent_ref[...]), unstack(total[...])
        nodes = nodes_ref[...]
        out_ref[...] = (
            part_ref[...]
            + split_dot(w1_ref[rows : 2 * rows, :], sent)
            + split_dot(w1_ref[2 * rows :, :], got)
        ).astype(BF16)
        rest_ref[:rows, :] = split_dot_nt(nodes, sent)
        rest_ref[rows:, :] = split_dot_nt(nodes, got)


def finish(returned, receivers, nodes, part, sent, w1, step):
    owners, rows, cap = returned.shape
    count = nodes.shape[1]
    slots = receivers.shape[1]
    whole = lambda a: pl.BlockSpec(a.shape, lambda i: (0,) * len(a.shape))
    outs = [
        jax.ShapeDtypeStruct((rows, count), BF16),
        jax.ShapeDtypeStruct((2 * rows, rows), F32),
    ]
    return pl.pallas_call(
        functools.partial(finish_kernel, cap),
        grid=(slots // step,),
        in_specs=[
            pl.BlockSpec((step // cap, rows, cap), lambda i: (i, 0, 0)),
            pl.BlockSpec((1, step), lambda i: (0, i)),
            *(whole(a) for a in (nodes, part, sent, w1)),
        ],
        out_specs=[whole(o) for o in outs],
        out_shape=outs,
        scratch_shapes=[pltpu.VMEM((rows * (count // LOW), LOW), F32)],
        compiler_params=pltpu.CompilerParams(vmem_limit_bytes=VMEM_LIMIT),
        name="sum_and_finish",
    )(returned, receivers, nodes, part, sent, w1)


def exchange(blocks):
    return lax.all_to_all(blocks, "edge", split_axis=0, concat_axis=0, tiled=True)


def per_device(
    nodes, edges, target, senders, receivers, counts, levels, land, channel_mask,
    edge_in, edge_in_bias, edge_out, edge_out_bias, edge_gain, edge_shift,
    node_in, node_in_bias, node_out, node_out_bias, node_gain, node_shift,
):
    rows, count = nodes.shape
    slots = edges.shape[1]
    owners = lax.axis_size("edge")
    step = min(2048, slots)
    levels_count = channel_mask.shape[0]
    cols = jnp.stack(
        [
            v.astype(F32)
            for v in (
                edge_in_bias, edge_out_bias, edge_gain, edge_shift,
                node_in_bias, node_out_bias, node_gain, node_shift,
                *(channel_mask[l] for l in range(levels_count)),
            )
        ],
        axis=1,
    )
    senders, receivers = senders.reshape(1, slots), receivers.reshape(1, slots)
    levels, land = levels.reshape(1, count), land.reshape(1, count)
    got = exchange(gather_for_owners(nodes, receivers, owners, step))
    message, pre, normal, inverse = edge_forward(
        counts, nodes, edges, got, senders, edge_in, edge_out, cols, step
    )
    new_nodes, part, agg_grad, node_first, node_second, node_vec = node_step(
        exchange(message), receivers, nodes, target, levels, land, node_in, node_out, cols,
        levels_count, step,
    )
    back = exchange(gather_for_owners(agg_grad, receivers, owners, step))
    edge_grad, pre_grad, sent, pair, edge_vec = edge_backward(
        counts, back, edges, pre, normal, inverse, senders, edge_in, edge_out, cols, count, step
    )
    node_grad, rest = finish(exchange(pre_grad), receivers, nodes, part, sent, edge_in, step)
    left = jnp.concatenate([pair[:rows, :rows], rest, pair[rows:, rows:]], axis=0)
    right = jnp.concatenate(
        [node_first, node_second, jnp.pad(jnp.concatenate([edge_vec, node_vec], 1), ((0, 0), (0, rows - 8)))],
        axis=0,
    )
    summed = lax.psum(jnp.concatenate([left, right], axis=1), ("edge", "rep"))
    left, right = summed[:, :rows], summed[:, rows:]
    vec = right[3 * rows :, :]
    return (
        new_nodes, node_grad, edge_grad,
        left[: 3 * rows], vec[:, 0], left[3 * rows :], vec[:, 1], vec[:, 2], vec[:, 3],
        right[: 2 * rows], vec[:, 4], right[2 * rows : 3 * rows], vec[:, 5], vec[:, 6], vec[:, 7],
    )


def solution(mesh):
    over = ("edge", "rep")
    wide, line, same = P(None, over), P(over), P()
    return jax.shard_map(
        per_device,
        mesh=mesh,
        in_specs=(wide, wide, wide, line, line, line, line, line) + (same,) * 13,
        out_specs=(wide, wide, wide) + (same,) * 12,
        check_vma=False,
    )
```

time: 732 us -> 456 us (0.62); the launches traced: 722 us -> 455 us
  matrix products: 244 us -> 0 us
  local copies, waits for them, and re-layouts: 236 us -> 13.4 us
  waiting for transfers between devices: 131 us -> 252 us
  Pallas kernels: 0 us -> 92.9 us
  other arithmetic: 60 us -> 1.63 us
  blocking collectives: 0 us -> 58.1 us
  starting transfers between devices: 35.7 us -> 22.7 us
    dot_general x37 -> x0, matrix products: 244 us -> none  [the longest x24 209 us: advance(): jnp.dot(piece_cols, one_hot, preferred_element_type=jnp.float32)]
    gather x3 -> x0, local copies, waits for them, and re-layouts: 172 us -> none  [the longest x1 57.4 us: per_device(): jnp.take(aggregate_grad, receivers, axis=1)]
    psum x1, waiting for transfers between devices: 19.6 us -> 127 us  [per_device(): summed = lax.psum(jnp.concatenate([left, right], axis=1), ('edge', 'rep'))]
    pallas_call x0 -> x6, Pallas kernels: none -> 92.9 us  [the longest x2 24.2 us: gather_for_owners(): pl.pallas_call(functools.partial(gather_kernel, cap), grid=(slots // step...]
    all_to_all x0 -> x1, blocking collectives: none -> 58.1 us  [exchange(): lax.all_to_all(blocks, 'edge', split_axis=0, concat_axis=0, tiled=True)]
    select_n x3 -> x0, other arithmetic: 34.5 us -> none  [the longest x1 11.5 us: per_device(): sender_cols = jnp.take(nodes, senders, axis=1)]
    all_to_all x7 -> x0, local copies, waits for them, and re-layouts: 22.2 us -> none  [the longest x2 9.66 us: per_device(): lax.all_to_all(owner_rows, 'edge', split_axis=1, concat_axis=1, tiled=True)]
    unnamed x97 -> x42, local copies, waits for them, and re-layouts: 28.9 us -> 6.91 us
  transfers between devices with their start and end apart: 5 -> 4, of which waited for: 4 -> 4; matrix products, arithmetic and copies ran while one was open for 24% -> 1% of each run, Pallas kernels for 0% -> 0%
where the time goes in v1:
time: 456 us; the launch traced here: 455 us
  waiting for transfers between devices  252 us (55%)
  Pallas kernels  92.9 us (20%)
  blocking collectives  58.1 us (13%)
  starting transfers between devices  22.7 us (5%)
  between operations  14.3 us (3%)
  local copies, waits for them, and re-layouts  13.4 us (3%)
    psum x1, waiting for transfers between devices, per_device(): summed = lax.psum(jnp.concatenate([left, right], axis=1), ('edge', 'rep'))  127 us
    all_to_all x3, waiting for transfers between devices, exchange(): lax.all_to_all(blocks, 'edge', split_axis=0, concat_axis=0, tiled=True)  125 us
    all_to_all x1, blocking collectives, exchange(): lax.all_to_all(blocks, 'edge', split_axis=0, concat_axis=0, tiled=True)  58.1 us
    pallas_call x2, Pallas kernels, gather_for_owners(): pl.pallas_call(functools.partial(gather_kernel, cap), grid=(slots // step...  24.2 us
    all_to_all x3, starting transfers between devices, exchange(): lax.all_to_all(blocks, 'edge', split_axis=0, concat_axis=0, tiled=True)  22.5 us
    pallas_call x1, Pallas kernels, edge_backward(): pl.pallas_call(functools.partial(edge_backward_kernel, cap, count), grid=...  20.7 us
    pallas_call x1, Pallas kernels, edge_forward(): pl.pallas_call(functools.partial(edge_forward_kernel, cap), grid=(slots /...  17.1 us
    pallas_call x1, Pallas kernels, node_step(): pl.pallas_call(functools.partial(node_kernel, cap, levels_count), grid=(s...  16.5 us
  transfers between devices with their start and end apart: 4, of which 4 were waited for; matrix products, arithmetic and copies ran while one was open for 1% of the time, Pallas kernels for 0%

profile of v1, /device:TPU:0, one launch (start us, length us, event | category | flops | bytes accessed | tf_op | source)
XLA Modules:
  0.0 454.8 jit_solution(3192295237249295235)
XLA Ops:
  7.2 12.1 %gather_columns.2 = bf16[16,64,1024]{2,1,0:T(8,128)(2,1)} custom-call(bf16[64,4096]{1,0:T(8,128)(2,1)} %nodes_ref.5, s32[1,16384]{1,0:T(1,128)} %bitcast.36), custom_call_target="tpu_custom_call" | custom-call | tf_op jit(solution)/shard_map/gather_columns/pallas_call | solution.py:124
  19.3 0.0 copy-start.14
  19.3 0.0 copy-start.15
  19.3 0.0 copy-start.16
  19.3 0.0 copy-start.17
  19.3 0.0 copy-start.18
  19.3 0.0 copy-start.10
  19.3 0.0 copy-start.6
  19.4 8.5 %all-to-all-start = ((bf16[16,64,1024]{2,1,0:T(8,128)(2,1)}), bf16[16,64,1024]{2,1,0:T(8,128)(2,1)S(1)}, u32[]{:S(2)}, u32[]{:S(2)}) async-start(bf16[16,64,1024]{2,1,0:T(8,128)(2,1)} %gather_columns.2), calls=%async_computation | async-start | bytes 4194304 | tf_op jit(solution)/shard_map/all_to_all | solution.py:412
  27.8 0.0 copy-done.11
  27.8 0.0 copy-done.12
  28.0 0.1 stack.71
  28.0 0.7 copy.73.cols_ref
  28.7 0.0 copy-done.6
  28.7 0.7 copy.72.w1_ref
  29.5 41.4 %all-to-all-done.got_ref = bf16[16,64,1024]{2,1,0:T(8,128)(2,1)S(1)} async-done(((bf16[16,64,1024]{2,1,0:T(8,128)(2,1)}), bf16[16,64,1024]{2,1,0:T(8,128)(2,1)S(1)}, u32[]{:S(2)}, u32[]{:S(2)}) %all-to-all-start) | async-done | bytes 2097184 | tf_op jit(solution)/shard_map/all_to_all | solution.py:412
  70.9 1.3 copy-done
  72.2 17.1 %edge_forward.1 = (bf16[16,64,1024]{2,1,0:T(8,128)(2,1)}, f32[64,16384]{1,0:T(8,128)}, f32[64,16384]{1,0:T(8,128)}, f32[1,16384]{1,0:T(1,128)}) custom-call(s32[16]{0:T(128)} %counts_ref.3, bf16[64,4096]{1,0:T(8,128)(2,1)} %nodes_ref.5, bf16[64,16384]{1,0:T(8,128)(2,1)} %edges_ref.3, bf16[16,64,1024]{2,1,0:T(8,128)(2,1)} %copy-done, s32[1,16384]{1,0:T(1,128)} %bitcast.40, ...), custom_call_target="tpu_custom_call" | custom-call | tf_op jit(solution)/shard_map/edge_forward/pallas_call | solution.py:184
  89.3 0.0 copy-start.9
  89.3 10.0 %all-to-all-start.1 = ((bf16[16,64,1024]{2,1,0:T(8,128)(2,1)}), bf16[16,64,1024]{2,1,0:T(8,128)(2,1)S(1)}, u32[]{:S(2)}, u32[]{:S(2)}) async-start(bf16[16,64,1024]{2,1,0:T(8,128)(2,1)} %get-tuple-element.32), calls=%async_computation.1 | async-start | bytes 4194304 | tf_op jit(solution)/shard_map/all_to_all | solution.py:412
  99.3 0.7 copy.74.w1_ref
  100.0 41.8 %all-to-all-done.1.arrived_ref = bf16[16,64,1024]{2,1,0:T(8,128)(2,1)S(1)} async-done(((bf16[16,64,1024]{2,1,0:T(8,128)(2,1)}), bf16[16,64,1024]{2,1,0:T(8,128)(2,1)S(1)}, u32[]{:S(2)}, u32[]{:S(2)}) %all-to-all-start.1) | async-done | bytes 2097184 | tf_op jit(solution)/shard_map/all_to_all | solution.py:412
  141.8 1.3 copy-done.2
  143.1 16.5 %sum_and_nodes.1 = (bf16[64,4096]{1,0:T(8,128)(2,1)}, f32[64,4096]{1,0:T(8,128)}, bf16[64,4096]{1,0:T(8,128)(2,1)}, f32[128,64]{1,0:T(8,128)}, f32[64,64]{1,0:T(8,128)}, /*index=5*/f32[64,4]{1,0:T(8,128)}) custom-call(bf16[16,64,1024]{2,1,0:T(8,128)(2,1)} %copy-done.2, s32[1,16384]{1,0:T(1,128)} %bitcast.37, bf16[64,4096]{1,0:T(8,128)(2,1)} %nodes_ref.5, ...), custom_call_target="tpu_custom_call" | custom-call | tf_op jit(solution)/shard_map/sum_and_nodes/pallas_call | solution.py:263
  159.6 12.1 %gather_columns.3 = bf16[16,64,1024]{2,1,0:T(8,128)(2,1)} custom-call(bf16[64,4096]{1,0:T(8,128)(2,1)} %get-tuple-element.34.table_ref, s32[1,16384]{1,0:T(1,128)} %bitcast.38), custom_call_target="tpu_custom_call" | custom-call | tf_op jit(solution)/shard_map/gather_columns/pallas_call | solution.py:124
  171.6 58.1 %all_to_all.20.back_ref = bf16[16,64,1024]{2,1,0:T(8,128)(2,1)} all-to-all(bf16[16,64,1024]{2,1,0:T(8,128)(2,1)} %gather_columns.3), channel_id=1, replica_groups=mesh['edge'=16,'rep'=2] {'edge'}, dimensions={0} | all-to-all | bytes 4194304 | tf_op jit(solution)/shard_map/all_to_all | solution.py:412
  229.7 20.7 %edge_backward.1 = (bf16[64,16384]{1,0:T(8,128)(2,1)}, bf16[16,64,1024]{2,1,0:T(8,128)(2,1)}, f32[1024,256]{1,0:T(8,128)}, f32[128,128]{1,0:T(8,128)}, f32[64,4]{1,0:T(8,128)}) custom-call(s32[16]{0:T(128)} %counts_ref.3, bf16[16,64,1024]{2,1,0:T(8,128)(2,1)} %all_to_all.20.back_ref, bf16[64,16384]{1,0:T(8,128)(2,1)} %edges_ref.3, ...), custom_call_target="tpu_custom_call" | custom-call | tf_op jit(solution)/shard_map/edge_backward/pallas_call | solution.py:332
  250.4 0.0 copy-start.8
  250.5 0.0 copy-start.3
  250.5 4.0 all-to-all-start.3
  254.5 0.2 all-reduce.3.cloned.1.call-start
  254.8 0.1 copy.80
  254.8 0.1 copy.79
  254.9 0.1 copy.81
  255.0 0.1 fusion.3
  255.1 41.9 %all-to-all-done.3.returned_ref = bf16[16,64,1024]{2,1,0:T(8,128)(2,1)S(1)} async-done(((bf16[16,64,1024]{2,1,0:T(8,128)(2,1)}), bf16[16,64,1024]{2,1,0:T(8,128)(2,1)S(1)}, u32[]{:S(2)}, u32[]{:S(2)}) %all-to-all-start.3) | async-done | bytes 2097184 | tf_op jit(solution)/shard_map/all_to_all | solution.py:412
  297.0 1.3 copy-done.1
  298.3 14.5 %sum_and_finish.1 = (bf16[64,4096]{1,0:T(8,128)(2,1)}, f32[128,64]{1,0:T(8,128)}) custom-call(bf16[16,64,1024]{2,1,0:T(8,128)(2,1)} %copy-done.1, s32[1,16384]{1,0:T(1,128)} %bitcast.39, bf16[64,4096]{1,0:T(8,128)(2,1)} %nodes_ref.5, f32[64,4096]{1,0:T(8,128)} %get-tuple-element.39.part_ref, f32[1024,256]{1,0:T(8,128)} %get-tuple-element.40.sent_ref, ...), custom_call_target="tpu_custom_call" | custom-call | tf_op jit(solution)/shard_map/sum_and_finish/pallas_call | solution.py:395
  312.8 0.0 copy-done.5
  312.8 1.6 fusion
  314.4 0.0 all-reduce.3.cloned.1.call-update
  314.4 126.7 %all-reduce.3.cloned.1.call-done = f32[256,128]{1,0:T(8,128)} async-done(((f32[256,128]{1,0:T(8,128)}), f32[256,128]{1,0:T(8,128)}) %all-reduce.3.cloned.1.call-update) | async-done | bytes 131088 | tf_op jit(solution)/shard_map/psum | solution.py:456
  441.1 0.9 slice.94
  442.0 0.7 copy.83
  442.8 0.9 slice.88
  443.6 0.7 copy.82
  444.4 2.1 slice_reduce_fusion
  446.5 1.5 fusion.2
  (27 shorter events, 0.1 us)
Async XLA Ops:
  19.3 8.6 %copy-start.11 = (bf16[64]{0:T(256)(128)(2,1)S(1)}, bf16[64]{0:T(256)(128)(2,1)}, u32[]{:S(2)}) copy-start(bf16[64]{0:T(256)(128)(2,1)} %param.33) | copy-start | bytes 388
  19.3 8.6 %copy-start.12 = (bf16[64]{0:T(256)(128)(2,1)S(1)}, bf16[64]{0:T(256)(128)(2,1)}, u32[]{:S(2)}) copy-start(bf16[64]{0:T(256)(128)(2,1)} %param.31) | copy-start | bytes 388
  19.3 8.6 %copy-start.13 = (bf16[64]{0:T(256)(128)(2,1)S(1)}, bf16[64]{0:T(256)(128)(2,1)}, u32[]{:S(2)}) copy-start(bf16[64]{0:T(256)(128)(2,1)} %param.35) | copy-start | bytes 388
  19.3 8.6 %copy-start.14 = (bf16[64]{0:T(256)(128)(2,1)S(1)}, bf16[64]{0:T(256)(128)(2,1)}, u32[]{:S(2)}) copy-start(bf16[64]{0:T(256)(128)(2,1)} %param.34) | copy-start | bytes 388
  19.3 8.6 %copy-start.15 = (bf16[64]{0:T(256)(128)(2,1)S(1)}, bf16[64]{0:T(256)(128)(2,1)}, u32[]{:S(2)}) copy-start(bf16[64]{0:T(256)(128)(2,1)} %param.39) | copy-start | bytes 388
  19.3 8.6 %copy-start.16 = (bf16[64]{0:T(256)(128)(2,1)S(1)}, bf16[64]{0:T(256)(128)(2,1)}, u32[]{:S(2)}) copy-start(bf16[64]{0:T(256)(128)(2,1)} %param.37) | copy-start | bytes 388
  19.3 8.6 %copy-start.17 = (bf16[64]{0:T(256)(128)(2,1)S(1)}, bf16[64]{0:T(256)(128)(2,1)}, u32[]{:S(2)}) copy-start(bf16[64]{0:T(256)(128)(2,1)} %param.41) | copy-start | bytes 388
  19.3 8.6 %copy-start.18 = (bf16[64]{0:T(256)(128)(2,1)S(1)}, bf16[64]{0:T(256)(128)(2,1)}, u32[]{:S(2)}) copy-start(bf16[64]{0:T(256)(128)(2,1)} %param.40) | copy-start | bytes 388
  19.3 8.6 %copy-start.10 = (s32[4,64]{1,0:T(4,128)S(1)}, s32[4,64]{1,0:T(4,128)}, u32[]{:S(2)}) copy-start(s32[4,64]{1,0:T(4,128)} %param.29) | copy-start | bytes 3076
  19.3 9.4 %copy-start.6 = (bf16[192,64]{0,1:T(8,128)(2,1)S(1)}, bf16[192,64]{0,1:T(8,128)(2,1)}, u32[]{:S(2)}) copy-start(bf16[192,64]{0,1:T(8,128)(2,1)} %param.30) | copy-start | bytes 73732
  19.4 51.5 %all-to-all-start = ((bf16[16,64,1024]{2,1,0:T(8,128)(2,1)}), bf16[16,64,1024]{2,1,0:T(8,128)(2,1)S(1)}, u32[]{:S(2)}, u32[]{:S(2)}) async-start(bf16[16,64,1024]{2,1,0:T(8,128)(2,1)} %gather_columns.2), calls=%async_computation | async-start | bytes 4194304 | tf_op jit(solution)/shard_map/all_to_all | solution.py:412
  70.9 1.3 copy-start
  89.3 10.0 %copy-start.9 = (bf16[128,64]{0,1:T(8,128)(2,1)S(1)}, bf16[128,64]{0,1:T(8,128)(2,1)}, u32[]{:S(2)}) copy-start(bf16[128,64]{0,1:T(8,128)(2,1)} %param.36) | copy-start | bytes 49156
  89.3 52.5 %all-to-all-start.1 = ((bf16[16,64,1024]{2,1,0:T(8,128)(2,1)}), bf16[16,64,1024]{2,1,0:T(8,128)(2,1)S(1)}, u32[]{:S(2)}, u32[]{:S(2)}) async-start(bf16[16,64,1024]{2,1,0:T(8,128)(2,1)} %get-tuple-element.32), calls=%async_computation.1 | async-start | bytes 4194304 | tf_op jit(solution)/shard_map/all_to_all | solution.py:412
  141.8 1.3 copy-start.2
  250.4 4.3 copy-start.7
  250.4 4.4 copy-start.8
  250.5 4.6 %copy-start.3 = (f32[128,128]{1,0:T(8,128)S(1)}, f32[128,128]{1,0:T(8,128)}, u32[]{:S(2)}) copy-start(f32[128,128]{1,0:T(8,128)} %get-tuple-element.43) | copy-start | bytes 196612
  250.5 46.5 %all-to-all-start.3 = ((bf16[16,64,1024]{2,1,0:T(8,128)(2,1)}), bf16[16,64,1024]{2,1,0:T(8,128)(2,1)S(1)}, u32[]{:S(2)}, u32[]{:S(2)}) async-start(bf16[16,64,1024]{2,1,0:T(8,128)(2,1)} %get-tuple-element.38), calls=%async_computation.3 | async-start | bytes 4194304 | tf_op jit(solution)/shard_map/all_to_all | solution.py:412
  254.5 186.6 %all-reduce.3.cloned.1.call-start = ((), (), s32[]{:S(2)}) async-start(), calls=%async_computation.4 | async-start | bytes 262144 | tf_op jit(solution)/shard_map/psum | solution.py:456
  297.0 1.3 copy-start.1
  298.3 14.5 %copy-start.4 = (f32[128,64]{1,0:T(8,128)S(1)}, f32[128,64]{1,0:T(8,128)}, u32[]{:S(2)}) copy-start(f32[128,64]{1,0:T(8,128)} %get-tuple-element.45) | copy-start | bytes 98308
  298.3 14.5 %copy-start.5 = (f32[64,64]{1,0:T(8,128)S(1)}, f32[64,64]{1,0:T(8,128)}, u32[]{:S(2)}) copy-start(f32[64,64]{1,0:T(8,128)} %get-tuple-element.46) | copy-start | bytes 49156
Sparse Core Ops, SparseCore 0:
  314.5 126.5 all-reduce.2

commit v2 on v1

v2 whole, which is shorter than its diff:
```python
import functools

import jax
import jax.numpy as jnp
from jax import lax
from jax.experimental import pallas as pl
from jax.experimental.pallas import tpu as pltpu
from jax.sharding import PartitionSpec as P

NORM_EPS = 1e-05
F32 = jnp.float32
BF16 = jnp.bfloat16
LOW = 256
VMEM_LIMIT = 60 * 2**20
PLANES = 4
MESH = pl.DeviceIdType.MESH

EB1, EB2, EG, EH, NB1, NB2, NG, NH, CM = 0, 1, 2, 3, 4, 5, 6, 7, 8


def dot(a, b):
    return jnp.dot(a, b, preferred_element_type=F32)


def dot_tn(a, b):
    return lax.dot_general(a, b, (((0,), (0,)), ((), ())), preferred_element_type=F32)


def dot_nt(a, b):
    return lax.dot_general(a, b, (((1,), (1,)), ((), ())), preferred_element_type=F32)


def one_hot_low(ids):
    low = ids & (LOW - 1)
    rows = lax.broadcasted_iota(jnp.int32, (LOW, ids.shape[1]), 0)
    return (rows == low).astype(F32).astype(BF16)


def high_of(ids, rows):
    high = ids >> (LOW.bit_length() - 1)
    return jnp.broadcast_to(high.astype(F32).astype(BF16), (rows, ids.shape[1]))


def stack_table(table_ref, value):
    rows = value.shape[0]
    for h in range(value.shape[1] // LOW):
        table_ref[h * rows : (h + 1) * rows, :] = value[:, h * LOW : (h + 1) * LOW]


def gather_columns(table, ids, rows):
    picked = dot(table, one_hot_low(ids)).astype(BF16)
    high = high_of(ids, rows)
    out = picked[:rows]
    for h in range(1, table.shape[0] // rows):
        out = jnp.where(high == BF16(h), picked[h * rows : (h + 1) * rows], out)
    return out


def scatter_columns(values, ids, count):
    rows = values.shape[0]
    high = high_of(ids, rows)
    zero = jnp.zeros_like(values)
    spread = jnp.concatenate(
        [jnp.where(high == BF16(h), values, zero) for h in range(count // LOW)], axis=0
    )
    return dot_nt(spread, one_hot_low(ids))


def column(cols, index):
    return cols[:, index : index + 1]


def mean_rows(v):
    return jnp.mean(v, axis=0, keepdims=True)


def lane_sums(v):
    out = v[:, :128]
    for k in range(1, v.shape[1] // 128):
        out = out + v[:, k * 128 : (k + 1) * 128]
    return out


def branch_forward(w1, w2, b1, b2, stacked):
    pre = dot_tn(w1, stacked) + b1
    hidden = (pre * (1.0 / (1.0 + jnp.exp(-pre)))).astype(BF16)
    outer = dot_tn(w2, hidden) + b2
    shifted = outer - mean_rows(outer)
    inverse = lax.rsqrt(mean_rows(shifted * shifted) + NORM_EPS)
    return pre, hidden, shifted * inverse, inverse


def branch_backward(w2, gain, grad, pre, normal, inverse):
    q = grad * gain
    outer_grad = (
        inverse * (q - mean_rows(q) - normal * mean_rows(q * normal))
    ).astype(BF16)
    s = 1.0 / (1.0 + jnp.exp(-pre))
    pre_grad = (dot(w2, outer_grad) * (s * (1.0 + pre * (1.0 - s)))).astype(BF16)
    return outer_grad, pre_grad, (pre * s).astype(BF16)


def split_dot(low, wide):
    top = wide.astype(BF16)
    rest = (wide - top.astype(F32)).astype(BF16)
    return dot(low, top) + dot(low, rest)


def layer_kernel(
    levels_count, reps,
    counts, nodes, edges, target, senders, receivers, levels, land, ew1, ew2, nw1, nw2, cols,
    new_nodes, node_grad, edge_grad, summed,
    tabs, send_a, recv_a, sent, ids_tab, pre_s, normal_s, inverse_s, send_b, recv_b, total,
    recv_c, recv_d, part, grads, sums, pieces,
    tab_send, tab_recv, ids_send, ids_recv, a_send, a_recv, b_send, b_recv,
    piece_send, piece_recv, sum_send, sum_recv,
):
    rows, count = nodes.shape
    owners, cap = senders.shape[0], senders.shape[2]
    ring = owners // PLANES
    high_count = count // LOW
    chunks = tab_recv.shape[2]
    chunk = tabs.shape[2] // chunks
    e, rep = lax.axis_index("edge"), lax.axis_index("rep")
    z, r = e // ring, e % ring
    me, devices = e * reps + rep, owners * reps
    upper = z // 2
    order = (z, z + 1 - 2 * upper, 2 - 2 * z + 5 * upper, 3 - 3 * upper)
    middle = lax.rem(z, 3) != 0
    toward = 3 - 2 * z

    def at(plane, place):
        return (plane * ring + place, rep)

    def remote(src, dst, send, recv, device):
        return pltpu.make_async_remote_copy(
            src, dst, send, recv, device_id=device, device_id_type=MESH
        )

    def loop(low, high, body):
        def step(i, carry):
            body(i)
            return carry

        lax.fori_loop(low, high, step, 0)

    def others(body):
        def one(t):
            d = lax.rem(me + t, devices)
            body(d, (d // reps, lax.rem(d, reps)))

        loop(1, devices, one)

    barrier = pltpu.get_barrier_semaphore()
    others(
        lambda d, device: pl.semaphore_signal(
            barrier, inc=1, device_id=device, device_id_type=MESH
        )
    )
    pl.semaphore_wait(barrier, devices - 1)

    def part_of(phase, plane, c):
        return tabs.at[phase, plane, pl.ds(c * chunk, chunk)]

    def table_copy(phase, plane, c, lane, to):
        return remote(
            part_of(phase, plane, c), part_of(phase, plane, c),
            tab_send.at[phase, lane, c], tab_recv.at[phase, plane, c], at(to, r),
        )

    def await_table(phase, plane, c):
        table_copy(phase, plane, c, 0, z).wait_recv()

    def send_own(phase, c):
        @pl.when(z < PLANES - 1)
        def _():
            table_copy(phase, z, c, 0, z + 1).start()

        @pl.when(z > 0)
        def _():
            table_copy(phase, z, c, 1, z - 1).start()

    def relay(phase, slot):
        @pl.when(middle)
        def _():
            for c in range(chunks):
                if slot == 0:
                    await_table(phase, z - toward, c)
                    table_copy(phase, z - toward, c, 2, z + toward).start()
                    await_table(phase, z + toward, c)
                    table_copy(phase, z + toward, c, 3, z - toward).start()
                else:
                    await_table(phase, z + 2 * toward, c)
                    table_copy(phase, z + 2 * toward, c, 4, z - toward).start()

    def end_wait(phase, k):
        @pl.when(jnp.logical_not(middle))
        def _():
            for c in range(chunks):
                await_table(phase, order[k], c)

    def drain_tables(phase):
        for c in range(chunks):
            @pl.when(z < PLANES - 1)
            def _():
                table_copy(phase, z, c, 0, z + 1).wait_send()

            @pl.when(z > 0)
            def _():
                table_copy(phase, z, c, 1, z - 1).wait_send()

            @pl.when(middle)
            def _():
                table_copy(phase, z - toward, c, 2, z + toward).wait_send()
                table_copy(phase, z + toward, c, 3, z - toward).wait_send()
                table_copy(phase, z + 2 * toward, c, 4, z - toward).wait_send()

    def ids_copy(k):
        plane = lax.rem(z + k, PLANES)
        return remote(
            receivers.at[pl.ds(plane * ring, ring)], ids_tab.at[pl.ds(z * ring, ring)],
            ids_send.at[plane], ids_recv.at[z], at(plane, r),
        )

    def ids_arrival(plane):
        rows_of = pl.ds(plane * ring, ring)
        return remote(
            ids_tab.at[rows_of], ids_tab.at[rows_of], ids_send.at[plane], ids_recv.at[plane],
            at(plane, r),
        )

    def plane_copy(phase, plane, to, into):
        return remote(
            send_a.at[plane * ring + to], into.at[plane * ring + r],
            a_send.at[phase, plane * ring + to], a_recv.at[phase, plane * ring + r], at(z, to),
        )

    def plane_arrival(phase, j, into):
        return remote(
            send_a.at[j], into.at[j], a_send.at[phase, j], a_recv.at[phase, j], at(z, r)
        )

    def gather_step(phase, k, into):
        plane = order[k]

        def one(t):
            to = lax.rem(r + t, ring)
            got = gather_columns(tabs[phase, plane], ids_tab[plane * ring + to], rows)

            @pl.when(t < ring)
            def _():
                send_a[plane * ring + to] = got
                plane_copy(phase, plane, to, into).start()

            @pl.when(t == ring)
            def _():
                into[plane * ring + r] = got

        loop(1, ring + 1, one)

    def drain_planes(phase, into):
        for plane in range(PLANES):
            loop(1, ring, lambda t: plane_copy(phase, plane, lax.rem(r + t, ring), into).wait_send())

    def direct_copy(phase, j, into):
        return remote(
            send_b.at[phase, j], into.at[e], b_send.at[phase, j], b_recv.at[phase, e], (j, rep)
        )

    def direct_arrival(phase, a, into):
        return remote(
            send_b.at[phase, a], into.at[a], b_send.at[phase, a], b_recv.at[phase, a], (e, rep)
        )

    def edge_step(phase, k, arrived, into, block):
        plane = order[k]

        def one(t):
            j = plane * ring + lax.rem(r + ring - t, ring)

            @pl.when(t > 0)
            def _():
                plane_arrival(phase, j, arrived).wait_recv()

            out = block(j)
            if k == 0:
                @pl.when(t == 0)
                def _():
                    into[e] = out

                @pl.when(t > 0)
                def _():
                    send_b[phase, j] = out
                    direct_copy(phase, j, into).start()
            else:
                send_b[phase, j] = out
                direct_copy(phase, j, into).start()

        loop(0, ring, one)

    def sum_arrived(phase, into):
        for k in range(PLANES):
            plane = order[k]

            def one(t):
                a = plane * ring + lax.rem(r + ring - t, ring)
                if k == 0:
                    @pl.when(t > 0)
                    def _():
                        direct_arrival(phase, a, into).wait_recv()
                else:
                    direct_arrival(phase, a, into).wait_recv()
                total[...] += scatter_columns(into[a], receivers[a], count)

            loop(0, ring, one)

    def drain_direct(phase, into):
        loop(1, owners, lambda t: direct_copy(phase, lax.rem(e + t, owners), into).wait_send())

    packed = cols[...]

    def lanes(j):
        return pl.ds(pl.multiple_of(j * cap, cap), cap)

    def live_of(j):
        place = lax.broadcasted_iota(jnp.int32, (1, cap), 1)
        return (place < counts[j]).astype(F32)

    def edge_forward(j):
        own = edges[:, lanes(j)]
        pre, _, normal, inverse = branch_forward(
            ew1[...], ew2[...], column(packed, EB1), column(packed, EB2),
            jnp.concatenate([own, sent[j], recv_a[j]], axis=0),
        )
        pre_s[j] = pre
        normal_s[j] = normal
        inverse_s[j] = inverse
        updated = own.astype(F32) + (normal * column(packed, EG) + column(packed, EH))
        return (updated * live_of(j)).astype(BF16)

    def edge_backward(j):
        grad = recv_c[j].astype(F32) * live_of(j)
        normal = normal_s[j]
        outer_grad, pre_grad, hidden = branch_backward(
            ew2[...], column(packed, EG), grad, pre_s[j], normal, inverse_s[j]
        )
        own = edges[:, lanes(j)]
        edge_grad[:, lanes(j)] = (grad + dot(ew1[:rows, :], pre_grad)).astype(BF16)
        grads[...] += dot_nt(
            jnp.concatenate([own, sent[j], recv_a[j], hidden], axis=0),
            jnp.concatenate([pre_grad, outer_grad], axis=0),
        )
        for k, v in enumerate((pre_grad.astype(F32), outer_grad.astype(F32), grad * normal, grad)):
            sums[k] += lane_sums(v)
        return pre_grad

    stack_table(tabs.at[0, z], nodes[...])
    for c in range(chunks):
        send_own(0, c)
    for k in range(1, PLANES):
        ids_copy(k).start()
    ids_tab[pl.ds(z * ring, ring)] = receivers[pl.ds(z * ring, ring)]
    total[...] = jnp.zeros_like(total)
    grads[...] = jnp.zeros_like(grads)
    sums[...] = jnp.zeros_like(sums)

    def senders_of(low, high):
        def one(j):
            sent[j] = gather_columns(tabs[0, z], senders[j], rows)

        loop(low, high, one)

    gather_step(0, 0, recv_a)
    senders_of(0, owners // 2)
    relay(0, 0)
    for k in range(1, PLANES):
        ids_arrival(order[k]).wait_recv()
    end_wait(0, 1)
    gather_step(0, 1, recv_a)
    senders_of(owners // 2, owners)
    edge_step(0, 0, recv_a, recv_b, edge_forward)
    relay(0, 1)
    end_wait(0, 2)
    gather_step(0, 2, recv_a)
    edge_step(0, 1, recv_a, recv_b, edge_forward)
    end_wait(0, 3)
    gather_step(0, 3, recv_a)
    edge_step(0, 2, recv_a, recv_b, edge_forward)
    edge_step(0, 3, recv_a, recv_b, edge_forward)
    for k in range(1, PLANES):
        ids_copy(k).wait_send()
    drain_planes(0, recv_a)
    sum_arrived(0, recv_b)

    per = high_count // chunks
    wide = per * LOW
    node_first = jnp.zeros((2 * rows, rows), F32)
    node_second = jnp.zeros((rows, rows), F32)
    node_sums = [jnp.zeros((rows, 128), F32)] * 4
    for c in range(chunks):
        here = slice(c * wide, (c + 1) * wide)
        aggregate = jnp.concatenate(
            [total[h * rows : (h + 1) * rows, :] for h in range(c * per, (c + 1) * per)], axis=1
        ).astype(BF16)
        own = nodes[:, here]
        stacked = jnp.concatenate([own, aggregate], axis=0)
        pre, _, normal, inverse = branch_forward(
            nw1[...], nw2[...], column(packed, NB1), column(packed, NB2), stacked
        )
        gain = column(packed, NG)
        state = own.astype(F32) + (normal * gain + column(packed, NH))
        new_nodes[:, here] = state.astype(BF16)
        weight = jnp.zeros((rows, wide), F32)
        for l in range(levels_count):
            weight = jnp.where(levels[:, here] == l, column(packed, CM + l), weight)
        weight = weight * land[:, here].astype(F32)
        grad = weight * (state - target[:, here].astype(F32))
        outer_grad, pre_grad, hidden = branch_backward(nw2[...], gain, grad, pre, normal, inverse)
        stacked_grad = dot(nw1[...], pre_grad)
        part[:, here] = grad + stacked_grad[:rows]
        low = stacked_grad[rows:].astype(BF16)
        for h in range(per):
            tabs[1, z, (c * per + h) * rows : (c * per + h + 1) * rows, :] = low[
                :, h * LOW : (h + 1) * LOW
            ]
        send_own(1, c)
        node_first = node_first + dot_nt(stacked, pre_grad)
        node_second = node_second + dot_nt(hidden, outer_grad)
        for k, v in enumerate((pre_grad.astype(F32), outer_grad.astype(F32), grad * normal, grad)):
            node_sums[k] = node_sums[k] + lane_sums(v)
    total[...] = jnp.zeros_like(total)

    gather_step(1, 0, recv_c)
    relay(1, 0)
    end_wait(1, 1)
    gather_step(1, 1, recv_c)
    edge_step(1, 0, recv_c, recv_d, edge_backward)
    relay(1, 1)
    end_wait(1, 2)
    gather_step(1, 2, recv_c)
    edge_step(1, 1, recv_c, recv_d, edge_backward)
    end_wait(1, 3)
    gather_step(1, 3, recv_c)
    edge_step(1, 2, recv_c, recv_d, edge_backward)
    edge_step(1, 3, recv_c, recv_d, edge_backward)

    grads[: 2 * rows, rows:] = node_first
    grads[2 * rows : 3 * rows, rows:] = node_second
    grads[3 * rows :, :8] = jnp.concatenate(
        [sums[k].sum(axis=1, keepdims=True) for k in range(4)]
        + [v.sum(axis=1, keepdims=True) for v in node_sums],
        axis=1,
    )
    reducers = min(devices, grads.shape[0] // 8)
    height = grads.shape[0] // reducers

    def piece(d):
        return pl.ds(pl.multiple_of(d * height, 8), height)

    def piece_copy(d, device):
        return remote(
            grads.at[piece(d)], pieces.at[me], piece_send.at[d], piece_recv.at[me], device
        )

    def piece_arrival(d):
        return remote(
            grads.at[piece(0)], pieces.at[d], piece_send.at[0], piece_recv.at[d], (e, rep)
        )

    def sum_copy(d, device):
        return remote(
            summed.at[piece(me)], summed.at[piece(me)], sum_send.at[d], sum_recv.at[me], device
        )

    def sum_arrival(d):
        return remote(
            summed.at[piece(d)], summed.at[piece(d)], sum_send.at[0], sum_recv.at[d], (e, rep)
        )

    def to_reducers(body):
        def one(d, device):
            if reducers == devices:
                body(d, device)
            else:
                @pl.when(d < reducers)
                def _():
                    body(d, device)

        others(one)

    def as_reducer(body):
        if reducers == devices:
            body()
        else:
            pl.when(me < reducers)(body)

    to_reducers(lambda d, device: piece_copy(d, device).start())

    def by_sender(j):
        @pl.when(j != e)
        def _():
            total[...] += scatter_columns(send_b[1, j], senders[j], count)

        @pl.when(j == e)
        def _():
            total[...] += scatter_columns(recv_d[e], senders[j], count)

    loop(0, owners, by_sender)

    @as_reducer
    def _():
        pieces[me] = grads[piece(me), :]
        others(lambda d, device: piece_arrival(d).wait_recv())

        def add(d, running):
            return running + pieces[d]

        summed[piece(me), :] = lax.fori_loop(
            1, devices, add, pieces[0]
        )
        others(lambda d, device: sum_copy(d, device).start())

    def node_total(w_rows):
        for h in range(high_count):
            here = slice(h * LOW, (h + 1) * LOW)
            part[:, here] += split_dot(ew1[w_rows, :], total[h * rows : (h + 1) * rows, :])

    node_total(slice(rows, 2 * rows))
    total[...] = jnp.zeros_like(total)
    sum_arrived(1, recv_d)
    node_total(slice(2 * rows, 3 * rows))
    node_grad[...] = part[...].astype(BF16)

    drain_tables(0)
    drain_direct(0, recv_b)
    drain_tables(1)
    drain_planes(1, recv_c)
    drain_direct(1, recv_d)
    to_reducers(lambda d, device: piece_copy(d, device).wait_send())

    @as_reducer
    def _():
        others(lambda d, device: sum_copy(d, device).wait_send())

    to_reducers(lambda d, device: sum_arrival(d).wait_recv())


def layer(
    counts, nodes, edges, target, senders, receivers, levels, land, ew1, ew2, nw1, nw2, cols,
    levels_count,
):
    rows, count = nodes.shape
    owners, _, cap = senders.shape
    slots = edges.shape[1]
    reps = lax.axis_size("rep")
    devices = owners * reps
    chunks = 4 if count // LOW % 4 == 0 else 1
    ring = owners // PLANES
    grad_shape = (4 * rows, 2 * rows)
    reducers = min(devices, grad_shape[0] // 8)
    blocks = (owners, rows, cap)
    dma = pltpu.SemaphoreType.DMA
    vmem = pl.BlockSpec(memory_space=pltpu.VMEM)
    return pl.pallas_call(
        functools.partial(layer_kernel, levels_count, reps),
        in_specs=[pl.BlockSpec(memory_space=pltpu.SMEM)] + [vmem] * 12,
        out_specs=[vmem] * 4,
        out_shape=[
            jax.ShapeDtypeStruct((rows, count), BF16),
            jax.ShapeDtypeStruct((rows, count), BF16),
            jax.ShapeDtypeStruct((rows, slots), BF16),
            jax.ShapeDtypeStruct(grad_shape, F32),
        ],
        scratch_shapes=[
            pltpu.VMEM((2, PLANES, rows * (count // LOW), LOW), BF16),
            pltpu.VMEM(blocks, BF16),
            pltpu.VMEM(blocks, BF16),
            pltpu.VMEM(blocks, BF16),
            pltpu.VMEM((owners, 1, cap), jnp.int32),
            pltpu.VMEM(blocks, F32),
            pltpu.VMEM(blocks, F32),
            pltpu.VMEM((owners, 1, cap), F32),
            pltpu.VMEM((2,) + blocks, BF16),
            pltpu.VMEM(blocks, BF16),
            pltpu.VMEM((rows * (count // LOW), LOW), F32),
            pltpu.VMEM(blocks, BF16),
            pltpu.VMEM(blocks, BF16),
            pltpu.VMEM((rows, count), F32),
            pltpu.VMEM(grad_shape, F32),
            pltpu.VMEM((4, rows, 128), F32),
            pltpu.VMEM((devices, grad_shape[0] // reducers, grad_shape[1]), F32),
            dma((2, 5, chunks)),
            dma((2, PLANES, chunks)),
            dma((PLANES,)),
            dma((PLANES,)),
            dma((2, owners)),
            dma((2, owners)),
            dma((2, owners)),
            dma((2, owners)),
            dma((reducers,)),
            dma((devices,)),
            dma((devices,)),
            dma((reducers,)),
        ],
        compiler_params=pltpu.CompilerParams(
            vmem_limit_bytes=VMEM_LIMIT, collective_id=0, has_side_effects=True
        ),
        cost_estimate=pl.CostEstimate(
            flops=64 * 2**30, bytes_accessed=16 * 2**20, transcendentals=4 * 2**20
        ),
        name="layer",
    )(counts, nodes, edges, target, senders, receivers, levels, land, ew1, ew2, nw1, nw2, cols)


def unpack_kernel(packed, *outs):
    rows = packed.shape[1] // 2
    lines = packed[3 * rows :, :].T
    edge_first, edge_b1, edge_second, edge_b2, edge_g, edge_h = outs[:6]
    node_first, node_b1, node_second, node_b2, node_g, node_h = outs[6:]
    edge_first[...] = packed[: 3 * rows, :rows]
    edge_second[...] = packed[3 * rows :, rows:]
    node_first[...] = packed[: 2 * rows, rows:]
    node_second[...] = packed[2 * rows : 3 * rows, rows:]
    for k, out in enumerate((edge_b1, edge_b2, edge_g, edge_h, node_b1, node_b2, node_g, node_h)):
        out[...] = lines[k, :rows]


def unpack(packed):
    rows = packed.shape[1] // 2
    vmem = pl.BlockSpec(memory_space=pltpu.VMEM)
    shapes = [
        (3 * rows, rows), (rows,), (rows, rows), (rows,), (rows,), (rows,),
        (2 * rows, rows), (rows,), (rows, rows), (rows,), (rows,), (rows,),
    ]
    return pl.pallas_call(
        unpack_kernel,
        in_specs=[vmem],
        out_specs=[vmem] * len(shapes),
        out_shape=[jax.ShapeDtypeStruct(s, F32) for s in shapes],
        name="unpack",
    )(packed)


def per_device(
    nodes, edges, target, senders, receivers, counts, levels, land, channel_mask,
    edge_in, edge_in_bias, edge_out, edge_out_bias, edge_gain, edge_shift,
    node_in, node_in_bias, node_out, node_out_bias, node_gain, node_shift,
):
    rows, count = nodes.shape
    slots = edges.shape[1]
    owners = lax.axis_size("edge")
    cap = slots // owners
    levels_count = channel_mask.shape[0]
    cols = jnp.stack(
        [
            v.astype(F32)
            for v in (
                edge_in_bias, edge_out_bias, edge_gain, edge_shift,
                node_in_bias, node_out_bias, node_gain, node_shift,
                *(channel_mask[l] for l in range(levels_count)),
            )
        ],
        axis=1,
    )
    new_nodes, node_grad, edge_grad, packed = layer(
        counts, nodes, edges, target,
        senders.reshape(owners, 1, cap), receivers.reshape(owners, 1, cap),
        levels.reshape(1, count), land.reshape(1, count),
        edge_in, edge_out, node_in, node_out, cols, levels_count,
    )
    return (new_nodes, node_grad, edge_grad, *unpack(packed))


def solution(mesh):
    over = ("edge", "rep")
    wide, line, same = P(None, over), P(over), P()
    return jax.shard_map(
        per_device,
        mesh=mesh,
        in_specs=(wide, wide, wide, line, line, line, line, line) + (same,) * 13,
        out_specs=(wide, wide, wide) + (same,) * 12,
        check_vma=False,
    )
```

time: 456 us -> 209 us (0.46)
  waiting for transfers between devices: 252 us -> 0 us
  Pallas kernels: 92.9 us -> 192 us
  blocking collectives: 58.1 us -> 0 us
  starting transfers between devices: 22.7 us -> 0 us
  between operations: 14.3 us -> 0.67 us
    psum x1 -> x0, waiting for transfers between devices: 127 us -> none  [per_device(): summed = lax.psum(jnp.concatenate([left, right], axis=1), ('edge', 'rep'))]
    all_to_all x3 -> x0, waiting for transfers between devices: 125 us -> none  [exchange(): lax.all_to_all(blocks, 'edge', split_axis=0, concat_axis=0, tiled=True)]
    pallas_call x6 -> x2, Pallas kernels: 92.9 us -> 192 us  [the longest x1 190 us: layer(): pl.pallas_call(functools.partial(layer_kernel, levels_count, reps), in_sp...]
    all_to_all x1 -> x0, blocking collectives: 58.1 us -> none  [exchange(): lax.all_to_all(blocks, 'edge', split_axis=0, concat_axis=0, tiled=True)]
    all_to_all x3 -> x0, starting transfers between devices: 22.5 us -> none  [exchange(): lax.all_to_all(blocks, 'edge', split_axis=0, concat_axis=0, tiled=True)]
    slice x5 -> x0, local copies, waits for them, and re-layouts: 5.46 us -> none  [the longest x1 2.1 us: per_device(): vec[:, 7]]
    unnamed x42 -> x9, local copies, waits for them, and re-layouts: 6.91 us -> 11.1 us
  transfers between devices with their start and end apart: 4 -> 0, of which waited for: 4 -> 0; matrix products, arithmetic and copies ran while one was open for 1% -> 0% of each run, Pallas kernels for 0% -> 0%
where the time goes in v2:
time: 209 us; the launch traced here: 208 us
  Pallas kernels  192 us (92%)
  local copies, waits for them, and re-layouts  11.9 us (6%)
  other arithmetic  3.53 us (2%)
    pallas_call x1, Pallas kernels, layer(): pl.pallas_call(functools.partial(layer_kernel, levels_count, reps), in_sp...  190 us
    unnamed x9, local copies, waits for them, and re-layouts  11.1 us

profile of v2, /device:TPU:0, one launch (start us, length us, event | category | flops | bytes accessed | tf_op | source)
XLA Modules:
  0.0 208.1 jit_solution(7303926469897097201)
XLA Ops:
  0.6 1.5 copy.52.ew1
  2.1 1.4 copy.53.nw1
  3.6 0.7 bitcast_convert_fusion.6
  4.2 0.7 bitcast_convert_fusion.4
  4.9 0.7 bitcast_convert_fusion.2
  5.6 0.7 bitcast_convert_fusion
  6.3 0.8 convert_bitcast_fusion
  7.1 0.7 copy.54.cols
  7.8 190.2 %layer.1 = (bf16[64,4096]{1,0:T(8,128)(2,1)}, bf16[64,4096]{1,0:T(8,128)(2,1)}, bf16[64,16384]{1,0:T(8,128)(2,1)}, f32[256,128]{1,0:T(8,128)}) custom-call(s32[16]{0:T(128)} %counts.1, bf16[64,4096]{1,0:T(8,128)(2,1)} %nodes.1, bf16[64,16384]{1,0:T(8,128)(2,1)} %edges.1, bf16[64,4096]{1,0:T(8,128)(2,1)} %target.1, s32[16,1,1024]{2,1,0:T(1,128)} %bitcast.36, ...), custom_call_target="tpu_custom_call" | custom-call | flops 68719476736 | bytes 16777216 | tf_op jit(solution)/shard_map/layer/pallas_call | solution.py:564
  198.1 0.0 copy-start
  198.1 1.8 unpack.1
  199.9 1.6 copy.55
  201.5 1.5 copy.56
  203.1 1.9 copy.60
  204.9 1.9 copy.61
  206.8 0.0 copy-done
  206.8 1.3 copy.62
  (1 shorter events, 0.0 us)
Async XLA Ops:
  198.1 8.7 %copy-start = (bf16[64,16384]{1,0:T(8,128)(2,1)S(1)}, bf16[64,16384]{1,0:T(8,128)(2,1)}, u32[]{:S(2)}) copy-start(bf16[64,16384]{1,0:T(8,128)(2,1)} %get-tuple-element.106) | copy-start | bytes 6291460

commit v3 on v2

--- a/solution.py
+++ b/solution.py
@@ -81,13 +81,13 @@
     return out
 
 
-def branch_forward(w1, w2, b1, b2, stacked):
-    pre = dot_tn(w1, stacked) + b1
+def branch_forward(w1t, w2t, b1, b2, stacked):
+    pre = dot(w1t, stacked) + b1
     hidden = (pre * (1.0 / (1.0 + jnp.exp(-pre)))).astype(BF16)
-    outer = dot_tn(w2, hidden) + b2
+    outer = dot(w2t, hidden) + b2
     shifted = outer - mean_rows(outer)
     inverse = lax.rsqrt(mean_rows(shifted * shifted) + NORM_EPS)
-    return pre, hidden, shifted * inverse, inverse
+    return pre, shifted * inverse, inverse
 
 
 def branch_backward(w2, gain, grad, pre, normal, inverse):
@@ -108,11 +108,12 @@
 
 def layer_kernel(
     levels_count, reps,
-    counts, nodes, edges, target, senders, receivers, levels, land, ew1, ew2, nw1, nw2, cols,
+    counts, nodes, edges, target, senders, receivers, levels, land, masks, ew1t, ew2, nw1t, nw2,
+    eb1, eb2, eg, eh, nb1, nb2, ng, nh,
     new_nodes, node_grad, edge_grad, summed,
-    tabs, send_a, recv_a, sent, ids_tab, pre_s, normal_s, inverse_s, send_b, recv_b, total,
-    recv_c, recv_d, part, grads, sums, pieces,
-    tab_send, tab_recv, ids_send, ids_recv, a_send, a_recv, b_send, b_recv,
+    tabs, send_a, recv_s, recv_e, mine, ids_tab, count_send, count_recv, pre_s, normal_s,
+    inverse_s, recv_c, send_d, recv_d, total, part, grads, sums, pieces, ew1, ew2t, nw1, nw2t, cols,
+    tab_send, tab_recv, ids_send, ids_recv, a_send, a_recv, b_send, b_recv, count_out, count_in,
     piece_send, piece_recv, sum_send, sum_recv,
 ):
     rows, count = nodes.shape
@@ -157,6 +158,24 @@
             barrier, inc=1, device_id=device, device_id_type=MESH
         )
     )
+
+    def eye(n):
+        return (
+            lax.broadcasted_iota(jnp.int32, (n, n), 0) == lax.broadcasted_iota(jnp.int32, (n, n), 1)
+        ).astype(F32).astype(BF16)
+
+    unit = eye(rows)
+    ew1[...] = dot_tn(ew1t[...], unit).astype(BF16)
+    nw1[...] = dot_tn(nw1t[...], unit).astype(BF16)
+    ew2t[...] = dot_tn(ew2[...], unit).astype(BF16)
+    nw2t[...] = dot_tn(nw2[...], unit).astype(BF16)
+    lines = [v[...].astype(F32)[None, :] for v in (eb1, eb2, eg, eh, nb1, nb2, ng, nh)]
+    lines.append(masks[...].astype(F32))
+    lines.append(jnp.zeros((-(8 + levels_count) % 16, rows), F32))
+    cols[...] = dot_nt(unit, jnp.concatenate(lines, axis=0).astype(BF16))
+    stack_table(tabs.at[0, z], nodes[...])
+    for j in range(owners):
+        count_send[j] = jnp.full(count_send.shape[1:], counts[j], jnp.int32)
     pl.semaphore_wait(barrier, devices - 1)
 
     def part_of(phase, plane, c):
@@ -215,18 +234,17 @@
                 table_copy(phase, z + toward, c, 3, z - toward).wait_send()
                 table_copy(phase, z + 2 * toward, c, 4, z - toward).wait_send()
 
-    def ids_copy(k):
+    def ids_copy(phase, ids, k):
         plane = lax.rem(z + k, PLANES)
         return remote(
-            receivers.at[pl.ds(plane * ring, ring)], ids_tab.at[pl.ds(z * ring, ring)],
-            ids_send.at[plane], ids_recv.at[z], at(plane, r),
-        )
-
-    def ids_arrival(plane):
-        rows_of = pl.ds(plane * ring, ring)
-        return remote(
-            ids_tab.at[rows_of], ids_tab.at[rows_of], ids_send.at[plane], ids_recv.at[plane],
-            at(plane, r),
+            ids.at[pl.ds(plane * ring, ring)], ids_tab.at[phase, pl.ds(z * ring, ring)],
+            ids_send.at[phase, plane], ids_recv.at[phase, z], at(plane, r),
+        )
+
+    def ids_arrival(phase, plane):
+        rows_of = ids_tab.at[phase, pl.ds(plane * ring, ring)]
+        return remote(
+            rows_of, rows_of, ids_send.at[phase, plane], ids_recv.at[phase, plane], at(plane, r)
         )
 
     def plane_copy(phase, plane, to, into):
@@ -240,21 +258,23 @@
             send_a.at[j], into.at[j], a_send.at[phase, j], a_recv.at[phase, j], at(z, r)
         )
 
+    def hand_over(phase, plane, to, t, got, into):
+        @pl.when(t < ring)
+        def _():
+            send_a[plane * ring + to] = got
+            plane_copy(phase, plane, to, into).start()
+
+        @pl.when(t == ring)
+        def _():
+            into[plane * ring + r] = got
+
     def gather_step(phase, k, into):
         plane = order[k]
 
         def one(t):
             to = lax.rem(r + t, ring)
-            got = gather_columns(tabs[phase, plane], ids_tab[plane * ring + to], rows)
-
-            @pl.when(t < ring)
-            def _():
-                send_a[plane * ring + to] = got
-                plane_copy(phase, plane, to, into).start()
-
-            @pl.when(t == ring)
-            def _():
-                into[plane * ring + r] = got
+            got = gather_columns(tabs[phase, plane], ids_tab[phase, plane * ring + to], rows)
+            hand_over(phase, plane, to, t, got, into)
 
         loop(1, ring + 1, one)
 
@@ -262,135 +282,163 @@
         for plane in range(PLANES):
             loop(1, ring, lambda t: plane_copy(phase, plane, lax.rem(r + t, ring), into).wait_send())
 
-    def direct_copy(phase, j, into):
-        return remote(
-            send_b.at[phase, j], into.at[e], b_send.at[phase, j], b_recv.at[phase, e], (j, rep)
-        )
-
-    def direct_arrival(phase, a, into):
-        return remote(
-            send_b.at[phase, a], into.at[a], b_send.at[phase, a], b_recv.at[phase, a], (e, rep)
-        )
-
-    def edge_step(phase, k, arrived, into, block):
-        plane = order[k]
-
+    def lanes(j):
+        return pl.ds(pl.multiple_of(j * cap, cap), cap)
+
+    def edges_copy(j):
+        return remote(
+            edges.at[:, lanes(j)], recv_e.at[e], b_send.at[0, j], b_recv.at[0, e], (j, rep)
+        )
+
+    def edges_arrival(a):
+        return remote(
+            edges.at[:, lanes(a)], recv_e.at[a], b_send.at[0, a], b_recv.at[0, a], (e, rep)
+        )
+
+    def count_copy(j):
+        return remote(
+            count_send.at[j], count_recv.at[e], count_out.at[j], count_in.at[e], (j, rep)
+        )
+
+    def count_arrival(a):
+        return remote(
+            count_send.at[a], count_recv.at[a], count_out.at[a], count_in.at[a], (e, rep)
+        )
+
+    def back_copy(a):
+        return remote(
+            send_d.at[a], recv_d.at[e], b_send.at[1, a], b_recv.at[1, e], (a, rep)
+        )
+
+    def back_arrival(j):
+        return remote(
+            send_d.at[j], recv_d.at[j], b_send.at[1, j], b_recv.at[1, j], (e, rep)
+        )
+
+    def peers(body):
+        loop(1, owners, lambda t: body(lax.rem(e + t, owners)))
+
+    def send_edges(k):
         def one(t):
-            j = plane * ring + lax.rem(r + ring - t, ring)
+            edges_copy(order[k] * ring + lax.rem(r + t, ring)).start()
+
+        loop(1 if k == 0 else 0, ring, one)
+
+    packed = cols[...]
+    place = lax.broadcasted_iota(jnp.int32, (1, cap), 1)
+
+    def live_here(a):
+        line = count_recv[a]
+        wide = jnp.concatenate([line] * (cap // line.shape[1]), axis=1)
+        return (place < wide).astype(F32)
+
+    def edge_forward(a):
+        own = recv_e[a]
+        pre, normal, inverse = branch_forward(
+            ew1t[...], ew2t[...], column(packed, EB1), column(packed, EB2),
+            jnp.concatenate([own, recv_s[a], mine[a]], axis=0),
+        )
+        pre_s[a] = pre
+        normal_s[a] = normal
+        inverse_s[a] = inverse
+        updated = own.astype(F32) + (normal * column(packed, EG) + column(packed, EH))
+        return (updated * live_here(a)).astype(BF16)
+
+    def forward_step(k):
+        def one(t):
+            a = order[k] * ring + lax.rem(r + ring - t, ring)
 
             @pl.when(t > 0)
             def _():
-                plane_arrival(phase, j, arrived).wait_recv()
-
-            out = block(j)
+                plane_arrival(0, a, recv_s).wait_recv()
+
             if k == 0:
-                @pl.when(t == 0)
-                def _():
-                    into[e] = out
-
                 @pl.when(t > 0)
                 def _():
-                    send_b[phase, j] = out
-                    direct_copy(phase, j, into).start()
+                    count_arrival(a).wait_recv()
+                    edges_arrival(a).wait_recv()
             else:
-                send_b[phase, j] = out
-                direct_copy(phase, j, into).start()
+                count_arrival(a).wait_recv()
+                edges_arrival(a).wait_recv()
+            total[...] += scatter_columns(edge_forward(a), receivers[a], count)
 
         loop(0, ring, one)
 
-    def sum_arrived(phase, into):
-        for k in range(PLANES):
-            plane = order[k]
-
-            def one(t):
-                a = plane * ring + lax.rem(r + ring - t, ring)
-                if k == 0:
-                    @pl.when(t > 0)
-                    def _():
-                        direct_arrival(phase, a, into).wait_recv()
-                else:
-                    direct_arrival(phase, a, into).wait_recv()
-                total[...] += scatter_columns(into[a], receivers[a], count)
-
-            loop(0, ring, one)
-
-    def drain_direct(phase, into):
-        loop(1, owners, lambda t: direct_copy(phase, lax.rem(e + t, owners), into).wait_send())
-
-    packed = cols[...]
-
-    def lanes(j):
-        return pl.ds(pl.multiple_of(j * cap, cap), cap)
-
-    def live_of(j):
-        place = lax.broadcasted_iota(jnp.int32, (1, cap), 1)
-        return (place < counts[j]).astype(F32)
-
-    def edge_forward(j):
-        own = edges[:, lanes(j)]
-        pre, _, normal, inverse = branch_forward(
-            ew1[...], ew2[...], column(packed, EB1), column(packed, EB2),
-            jnp.concatenate([own, sent[j], recv_a[j]], axis=0),
-        )
-        pre_s[j] = pre
-        normal_s[j] = normal
-        inverse_s[j] = inverse
-        updated = own.astype(F32) + (normal * column(packed, EG) + column(packed, EH))
-        return (updated * live_of(j)).astype(BF16)
-
-    def edge_backward(j):
-        grad = recv_c[j].astype(F32) * live_of(j)
-        normal = normal_s[j]
+    def edge_backward(a, got):
+        grad = got.astype(F32) * live_here(a)
+        normal = normal_s[a]
         outer_grad, pre_grad, hidden = branch_backward(
-            ew2[...], column(packed, EG), grad, pre_s[j], normal, inverse_s[j]
-        )
-        own = edges[:, lanes(j)]
-        edge_grad[:, lanes(j)] = (grad + dot(ew1[:rows, :], pre_grad)).astype(BF16)
+            ew2[...], column(packed, EG), grad, pre_s[a], normal, inverse_s[a]
+        )
         grads[...] += dot_nt(
-            jnp.concatenate([own, sent[j], recv_a[j], hidden], axis=0),
+            jnp.concatenate([recv_e[a], recv_s[a], mine[a], hidden], axis=0),
             jnp.concatenate([pre_grad, outer_grad], axis=0),
         )
         for k, v in enumerate((pre_grad.astype(F32), outer_grad.astype(F32), grad * normal, grad)):
             sums[k] += lane_sums(v)
         return pre_grad
 
-    stack_table(tabs.at[0, z], nodes[...])
+    def backward_step(k):
+        plane = order[k]
+
+        def one(t):
+            to = lax.rem(r + t, ring)
+            a = plane * ring + to
+            got = gather_columns(tabs[1, z], receivers[a], rows)
+            if k == 0:
+                hand_over(1, z, to, t, got, recv_c)
+            pre_grad = edge_backward(a, got)
+            send_d[a] = pre_grad
+            if k == 0:
+                @pl.when(t < ring)
+                def _():
+                    back_copy(a).start()
+            else:
+                back_copy(a).start()
+
+        loop(1, ring + 1, one)
+
     for c in range(chunks):
         send_own(0, c)
     for k in range(1, PLANES):
-        ids_copy(k).start()
-    ids_tab[pl.ds(z * ring, ring)] = receivers[pl.ds(z * ring, ring)]
+        ids_copy(0, senders, k).start()
+    peers(lambda j: count_copy(j).start())
+    send_edges(0)
+    send_edges(1)
+    ids_tab[0, pl.ds(z * ring, ring)] = senders[pl.ds(z * ring, ring)]
+    count_recv[e] = count_send[e]
+    recv_e[e] = edges[:, lanes(e)]
     total[...] = jnp.zeros_like(total)
     grads[...] = jnp.zeros_like(grads)
     sums[...] = jnp.zeros_like(sums)
 
-    def senders_of(low, high):
-        def one(j):
-            sent[j] = gather_columns(tabs[0, z], senders[j], rows)
+    def mine_of(low, high):
+        def one(a):
+            mine[a] = gather_columns(tabs[0, z], receivers[a], rows)
 
         loop(low, high, one)
 
-    gather_step(0, 0, recv_a)
-    senders_of(0, owners // 2)
+    gather_step(0, 0, recv_s)
+    mine_of(0, owners // 2)
     relay(0, 0)
     for k in range(1, PLANES):
-        ids_arrival(order[k]).wait_recv()
+        ids_arrival(0, order[k]).wait_recv()
     end_wait(0, 1)
-    gather_step(0, 1, recv_a)
-    senders_of(owners // 2, owners)
-    edge_step(0, 0, recv_a, recv_b, edge_forward)
+    gather_step(0, 1, recv_s)
+    send_edges(2)
+    mine_of(owners // 2, owners)
     relay(0, 1)
     end_wait(0, 2)
-    gather_step(0, 2, recv_a)
-    edge_step(0, 1, recv_a, recv_b, edge_forward)
+    gather_step(0, 2, recv_s)
+    send_edges(3)
+    forward_step(0)
     end_wait(0, 3)
-    gather_step(0, 3, recv_a)
-    edge_step(0, 2, recv_a, recv_b, edge_forward)
-    edge_step(0, 3, recv_a, recv_b, edge_forward)
+    gather_step(0, 3, recv_s)
     for k in range(1, PLANES):
-        ids_copy(k).wait_send()
-    drain_planes(0, recv_a)
-    sum_arrived(0, recv_b)
+        ids_copy(1, receivers, k).start()
+    for k in range(1, PLANES):
+        forward_step(k)
+    drain_planes(0, recv_s)
 
     per = high_count // chunks
     wide = per * LOW
@@ -404,8 +452,8 @@
         ).astype(BF16)
         own = nodes[:, here]
         stacked = jnp.concatenate([own, aggregate], axis=0)
-        pre, _, normal, inverse = branch_forward(
-            nw1[...], nw2[...], column(packed, NB1), column(packed, NB2), stacked
+        pre, normal, inverse = branch_forward(
+            nw1t[...], nw2t[...], column(packed, NB1), column(packed, NB2), stacked
         )
         gain = column(packed, NG)
         state = own.astype(F32) + (normal * gain + column(packed, NH))
@@ -428,21 +476,19 @@
         node_second = node_second + dot_nt(hidden, outer_grad)
         for k, v in enumerate((pre_grad.astype(F32), outer_grad.astype(F32), grad * normal, grad)):
             node_sums[k] = node_sums[k] + lane_sums(v)
-    total[...] = jnp.zeros_like(total)
-
-    gather_step(1, 0, recv_c)
+
+    backward_step(0)
+    backward_step(1)
     relay(1, 0)
+    for k in range(1, PLANES):
+        ids_arrival(1, order[k]).wait_recv()
     end_wait(1, 1)
     gather_step(1, 1, recv_c)
-    edge_step(1, 0, recv_c, recv_d, edge_backward)
+    backward_step(2)
     relay(1, 1)
     end_wait(1, 2)
     gather_step(1, 2, recv_c)
-    edge_step(1, 1, recv_c, recv_d, edge_backward)
-    end_wait(1, 3)
-    gather_step(1, 3, recv_c)
-    edge_step(1, 2, recv_c, recv_d, edge_backward)
-    edge_step(1, 3, recv_c, recv_d, edge_backward)
+    backward_step(3)
 
     grads[: 2 * rows, rows:] = node_first
     grads[2 * rows : 3 * rows, rows:] = node_second
@@ -495,17 +541,23 @@
             pl.when(me < reducers)(body)
 
     to_reducers(lambda d, device: piece_copy(d, device).start())
-
-    def by_sender(j):
-        @pl.when(j != e)
-        def _():
-            total[...] += scatter_columns(send_b[1, j], senders[j], count)
-
-        @pl.when(j == e)
-        def _():
-            total[...] += scatter_columns(recv_d[e], senders[j], count)
-
-    loop(0, owners, by_sender)
+    end_wait(1, 3)
+    gather_step(1, 3, recv_c)
+
+    total[...] = jnp.zeros_like(total)
+
+    def by_receiver(a):
+        total[...] += scatter_columns(send_d[a], receivers[a], count)
+
+    loop(0, owners, by_receiver)
+
+    def node_total(w_rows):
+        for h in range(high_count):
+            here = slice(h * LOW, (h + 1) * LOW)
+            part[:, here] += split_dot(ew1[w_rows, :], total[h * rows : (h + 1) * rows, :])
+
+    node_total(slice(2 * rows, 3 * rows))
+    total[...] = jnp.zeros_like(total)
 
     @as_reducer
     def _():
@@ -515,27 +567,40 @@
         def add(d, running):
             return running + pieces[d]
 
-        summed[piece(me), :] = lax.fori_loop(
-            1, devices, add, pieces[0]
-        )
+        summed[piece(me), :] = lax.fori_loop(1, devices, add, pieces[0])
         others(lambda d, device: sum_copy(d, device).start())
 
-    def node_total(w_rows):
-        for h in range(high_count):
-            here = slice(h * LOW, (h + 1) * LOW)
-            part[:, here] += split_dot(ew1[w_rows, :], total[h * rows : (h + 1) * rows, :])
-
+    def finish_block(j, pre_grad):
+        grad = recv_c[j].astype(F32) * (place < counts[j]).astype(F32)
+        edge_grad[:, lanes(j)] = (grad + dot(ew1[:rows, :], pre_grad)).astype(BF16)
+        total[...] += scatter_columns(pre_grad, senders[j], count)
+
+    finish_block(e, send_d[e])
+    for k in range(PLANES):
+        def one(t):
+            j = order[k] * ring + lax.rem(r + ring - t, ring)
+            if k == 0:
+                plane_arrival(1, j, recv_c).wait_recv()
+            else:
+                @pl.when(t > 0)
+                def _():
+                    plane_arrival(1, j, recv_c).wait_recv()
+            back_arrival(j).wait_recv()
+            finish_block(j, recv_d[j])
+
+        loop(1 if k == 0 else 0, ring, one)
     node_total(slice(rows, 2 * rows))
-    total[...] = jnp.zeros_like(total)
-    sum_arrived(1, recv_d)
-    node_total(slice(2 * rows, 3 * rows))
     node_grad[...] = part[...].astype(BF16)
 
     drain_tables(0)
-    drain_direct(0, recv_b)
     drain_tables(1)
     drain_planes(1, recv_c)
-    drain_direct(1, recv_d)
+    for k in range(1, PLANES):
+        ids_copy(0, senders, k).wait_send()
+        ids_copy(1, receivers, k).wait_send()
+    peers(lambda j: count_copy(j).wait_send())
+    peers(lambda j: edges_copy(j).wait_send())
+    peers(lambda j: back_copy(j).wait_send())
     to_reducers(lambda d, device: piece_copy(d, device).wait_send())
 
     @as_reducer
@@ -545,25 +610,21 @@
     to_reducers(lambda d, device: sum_arrival(d).wait_recv())
 
 
-def layer(
-    counts, nodes, edges, target, senders, receivers, levels, land, ew1, ew2, nw1, nw2, cols,
-    levels_count,
-):
+def layer(counts, nodes, edges, target, senders, receivers, levels, land, masks, *weights):
     rows, count = nodes.shape
     owners, _, cap = senders.shape
     slots = edges.shape[1]
     reps = lax.axis_size("rep")
     devices = owners * reps
     chunks = 4 if count // LOW % 4 == 0 else 1
-    ring = owners // PLANES
     grad_shape = (4 * rows, 2 * rows)
     reducers = min(devices, grad_shape[0] // 8)
     blocks = (owners, rows, cap)
     dma = pltpu.SemaphoreType.DMA
     vmem = pl.BlockSpec(memory_space=pltpu.VMEM)
     return pl.pallas_call(
-        functools.partial(layer_kernel, levels_count, reps),
-        in_specs=[pl.BlockSpec(memory_space=pltpu.SMEM)] + [vmem] * 12,
+        functools.partial(layer_kernel, masks.shape[0], reps),
+        in_specs=[pl.BlockSpec(memory_space=pltpu.SMEM)] + [vmem] * (8 + len(weights)),
         out_specs=[vmem] * 4,
         out_shape=[
             jax.ShapeDtypeStruct((rows, count), BF16),
@@ -576,27 +637,36 @@
             pltpu.VMEM(blocks, BF16),
             pltpu.VMEM(blocks, BF16),
             pltpu.VMEM(blocks, BF16),
-            pltpu.VMEM((owners, 1, cap), jnp.int32),
+            pltpu.VMEM(blocks, BF16),
+            pltpu.VMEM((2, owners, 1, cap), jnp.int32),
+            pltpu.VMEM((owners, 1, 128), jnp.int32),
+            pltpu.VMEM((owners, 1, 128), jnp.int32),
             pltpu.VMEM(blocks, F32),
             pltpu.VMEM(blocks, F32),
             pltpu.VMEM((owners, 1, cap), F32),
-            pltpu.VMEM((2,) + blocks, BF16),
+            pltpu.VMEM(blocks, BF16),
+            pltpu.VMEM(blocks, BF16),
             pltpu.VMEM(blocks, BF16),
             pltpu.VMEM((rows * (count // LOW), LOW), F32),
-            pltpu.VMEM(blocks, BF16),
-            pltpu.VMEM(blocks, BF16),
             pltpu.VMEM((rows, count), F32),
             pltpu.VMEM(grad_shape, F32),
             pltpu.VMEM((4, rows, 128), F32),
             pltpu.VMEM((devices, grad_shape[0] // reducers, grad_shape[1]), F32),
+            pltpu.VMEM((3 * rows, rows), BF16),
+            pltpu.VMEM((rows, rows), BF16),
+            pltpu.VMEM((2 * rows, rows), BF16),
+            pltpu.VMEM((rows, rows), BF16),
+            pltpu.VMEM((rows, 16 * -(-(8 + masks.shape[0]) // 16)), F32),
             dma((2, 5, chunks)),
             dma((2, PLANES, chunks)),
-            dma((PLANES,)),
-            dma((PLANES,)),
+            dma((2, PLANES)),
+            dma((2, PLANES)),
             dma((2, owners)),
             dma((2, owners)),
             dma((2, owners)),
             dma((2, owners)),
+            dma((owners,)),
+            dma((owners,)),
             dma((reducers,)),
             dma((devices,)),
             dma((devices,)),
@@ -609,36 +679,54 @@
             flops=64 * 2**30, bytes_accessed=16 * 2**20, transcendentals=4 * 2**20
         ),
         name="layer",
-    )(counts, nodes, edges, target, senders, receivers, levels, land, ew1, ew2, nw1, nw2, cols)
-
-
-def unpack_kernel(packed, *outs):
+    )(counts, nodes, edges, target, senders, receivers, levels, land, masks, *weights)
+
+
+def hand_out_kernel(new_in, node_in, edge_in, packed, new_nodes, node_grad, edge_grad, *rest):
+    outs, sems = rest[:-1], rest[-1]
+    copies = [
+        pltpu.make_async_copy(src, dst, sems.at[k])
+        for k, (src, dst) in enumerate(
+            ((edge_in, edge_grad), (new_in, new_nodes), (node_in, node_grad))
+        )
+    ]
+    for copy in copies:
+        copy.start()
     rows = packed.shape[1] // 2
     lines = packed[3 * rows :, :].T
     edge_first, edge_b1, edge_second, edge_b2, edge_g, edge_h = outs[:6]
     node_first, node_b1, node_second, node_b2, node_g, node_h = outs[6:]
-    edge_first[...] = packed[: 3 * rows, :rows]
+    edge_first[...] = packed[: 3 * rows, :].T[:rows, :]
     edge_second[...] = packed[3 * rows :, rows:]
-    node_first[...] = packed[: 2 * rows, rows:]
+    node_first[...] = packed[: 2 * rows, :].T[rows:, :]
     node_second[...] = packed[2 * rows : 3 * rows, rows:]
     for k, out in enumerate((edge_b1, edge_b2, edge_g, edge_h, node_b1, node_b2, node_g, node_h)):
         out[...] = lines[k, :rows]
-
-
-def unpack(packed):
+    for copy in copies:
+        copy.wait()
+
+
+def hand_out(new_nodes, node_grad, edge_grad, packed):
     rows = packed.shape[1] // 2
     vmem = pl.BlockSpec(memory_space=pltpu.VMEM)
+    stay = pl.BlockSpec(memory_space=pl.ANY)
     shapes = [
-        (3 * rows, rows), (rows,), (rows, rows), (rows,), (rows,), (rows,),
-        (2 * rows, rows), (rows,), (rows, rows), (rows,), (rows,), (rows,),
+        (rows, 3 * rows), (rows,), (rows, rows), (rows,), (rows,), (rows,),
+        (rows, 2 * rows), (rows,), (rows, rows), (rows,), (rows,), (rows,),
     ]
-    return pl.pallas_call(
-        unpack_kernel,
-        in_specs=[vmem],
-        out_specs=[vmem] * len(shapes),
-        out_shape=[jax.ShapeDtypeStruct(s, F32) for s in shapes],
-        name="unpack",
-    )(packed)
+    large = [jax.ShapeDtypeStruct(a.shape, a.dtype) for a in (new_nodes, node_grad, edge_grad)]
+    outs = pl.pallas_call(
+        hand_out_kernel,
+        in_specs=[stay] * 3 + [vmem],
+        out_specs=[stay] * 3 + [vmem] * len(shapes),
+        out_shape=large + [jax.ShapeDtypeStruct(s, F32) for s in shapes],
+        scratch_shapes=[pltpu.SemaphoreType.DMA((3,))],
+        compiler_params=pltpu.CompilerParams(vmem_limit_bytes=VMEM_LIMIT),
+        name="hand_out",
+    )(new_nodes, node_grad, edge_grad, packed)
+    outs = list(outs)
+    outs[3], outs[9] = outs[3].T, outs[9].T
+    return tuple(outs)
 
 
 def per_device(
@@ -646,29 +734,19 @@
     edge_in, edge_in_bias, edge_out, edge_out_bias, edge_gain, edge_shift,
     node_in, node_in_bias, node_out, node_out_bias, node_gain, node_shift,
 ):
-    rows, count = nodes.shape
-    slots = edges.shape[1]
+    count = nodes.shape[1]
     owners = lax.axis_size("edge")
-    cap = slots // owners
-    levels_count = channel_mask.shape[0]
-    cols = jnp.stack(
-        [
-            v.astype(F32)
-            for v in (
-                edge_in_bias, edge_out_bias, edge_gain, edge_shift,
-                node_in_bias, node_out_bias, node_gain, node_shift,
-                *(channel_mask[l] for l in range(levels_count)),
-            )
-        ],
-        axis=1,
+    cap = edges.shape[1] // owners
+    return hand_out(
+        *layer(
+            counts, nodes, edges, target,
+            senders.reshape(owners, 1, cap), receivers.reshape(owners, 1, cap),
+            levels.reshape(1, count), land.reshape(1, count), channel_mask,
+            edge_in.T, edge_out, node_in.T, node_out,
+            edge_in_bias, edge_out_bias, edge_gain, edge_shift,
+            node_in_bias, node_out_bias, node_gain, node_shift,
+        )
     )
-    new_nodes, node_grad, edge_grad, packed = layer(
-        counts, nodes, edges, target,
-        senders.reshape(owners, 1, cap), receivers.reshape(owners, 1, cap),
-        levels.reshape(1, count), land.reshape(1, count),
-        edge_in, edge_out, node_in, node_out, cols, levels_count,
-    )
-    return (new_nodes, node_grad, edge_grad, *unpack(packed))
 
 
 def solution(mesh):

time: 209 us -> 314 us (1.50)
  Pallas kernels: 192 us -> 313 us
  local copies, waits for them, and re-layouts: 11.9 us -> 0 us
  other arithmetic: 3.53 us -> 0 us
    pallas_call x2, Pallas kernels: 192 us -> 313 us  [the longest x1 215 us: layer(): pl.pallas_call(functools.partial(layer_kernel, masks.shape[0], reps), in_...]
    unnamed x9 -> x0, local copies, waits for them, and re-layouts: 11.1 us -> none
where the time goes in v3:
time: 314 us
  Pallas kernels  313 us (100%)
    pallas_call x1, Pallas kernels, layer(): pl.pallas_call(functools.partial(layer_kernel, masks.shape[0], reps), in_...  215 us
    pallas_call x1, Pallas kernels, hand_out(): pl.pallas_call(hand_out_kernel, in_specs=[stay] * 3 + [vmem], out_specs=[...  98 us

profile of v3, /device:TPU:0, one launch (start us, length us, event | category | flops | bytes accessed | tf_op | source)
XLA Modules:
  0.0 313.5 jit_solution(1333723199697671903)
XLA Ops:
  0.7 214.7 %layer.1 = (bf16[64,4096]{1,0:T(8,128)(2,1)}, bf16[64,4096]{1,0:T(8,128)(2,1)}, bf16[64,16384]{1,0:T(8,128)(2,1)}, f32[256,128]{1,0:T(8,128)}) custom-call(s32[16]{0:T(128)} %counts.1, bf16[64,4096]{1,0:T(8,128)(2,1)} %nodes.1, bf16[64,16384]{1,0:T(8,128)(2,1)} %edges.1, bf16[64,4096]{1,0:T(8,128)(2,1)} %target.1, s32[16,1,1024]{2,1,0:T(1,128)} %bitcast.8, ...), custom_call_target="tpu_custom_call" | custom-call | flops 68719476736 | bytes 16777216 | tf_op jit(solution)/shard_map/layer/pallas_call | solution.py:625
  215.3 98.0 %hand_out.1 = (bf16[64,4096]{1,0:T(8,128)(2,1)}, bf16[64,4096]{1,0:T(8,128)(2,1)}, bf16[64,16384]{1,0:T(8,128)(2,1)}, f32[64,192]{1,0:T(8,128)}, f32[64]{0:T(128...) custom-call(bf16[64,4096]{1,0:T(8,128)(2,1)} %get-tuple-element.34.n, ...), custom_call_target="tpu_custom_call" | custom-call | tf_op jit(solution)/shard_map/hand_out/pallas_call | solution.py:718

commit v4 on v3

--- a/solution.py
+++ b/solution.py
@@ -395,6 +395,7 @@
                     back_copy(a).start()
             else:
                 back_copy(a).start()
+            total[...] += scatter_columns(pre_grad, receivers[a], count)
 
         loop(1, ring + 1, one)
 
@@ -404,7 +405,6 @@
         ids_copy(0, senders, k).start()
     peers(lambda j: count_copy(j).start())
     send_edges(0)
-    send_edges(1)
     ids_tab[0, pl.ds(z * ring, ring)] = senders[pl.ds(z * ring, ring)]
     count_recv[e] = count_send[e]
     recv_e[e] = edges[:, lanes(e)]
@@ -424,15 +424,16 @@
     for k in range(1, PLANES):
         ids_arrival(0, order[k]).wait_recv()
     end_wait(0, 1)
+    send_edges(1)
     gather_step(0, 1, recv_s)
-    send_edges(2)
     mine_of(owners // 2, owners)
     relay(0, 1)
     end_wait(0, 2)
+    send_edges(2)
     gather_step(0, 2, recv_s)
-    send_edges(3)
     forward_step(0)
     end_wait(0, 3)
+    send_edges(3)
     gather_step(0, 3, recv_s)
     for k in range(1, PLANES):
         ids_copy(1, receivers, k).start()
@@ -477,17 +478,20 @@
         for k, v in enumerate((pre_grad.astype(F32), outer_grad.astype(F32), grad * normal, grad)):
             node_sums[k] = node_sums[k] + lane_sums(v)
 
+    total[...] = jnp.zeros_like(total)
     backward_step(0)
-    backward_step(1)
     relay(1, 0)
     for k in range(1, PLANES):
         ids_arrival(1, order[k]).wait_recv()
     end_wait(1, 1)
     gather_step(1, 1, recv_c)
-    backward_step(2)
+    backward_step(1)
     relay(1, 1)
     end_wait(1, 2)
     gather_step(1, 2, recv_c)
+    backward_step(2)
+    end_wait(1, 3)
+    gather_step(1, 3, recv_c)
     backward_step(3)
 
     grads[: 2 * rows, rows:] = node_first
@@ -541,16 +545,6 @@
             pl.when(me < reducers)(body)
 
     to_reducers(lambda d, device: piece_copy(d, device).start())
-    end_wait(1, 3)
-    gather_step(1, 3, recv_c)
-
-    total[...] = jnp.zeros_like(total)
-
-    def by_receiver(a):
-        total[...] += scatter_columns(send_d[a], receivers[a], count)
-
-    loop(0, owners, by_receiver)
-
     def node_total(w_rows):
         for h in range(high_count):
             here = slice(h * LOW, (h + 1) * LOW)
@@ -682,15 +676,19 @@
     )(counts, nodes, edges, target, senders, receivers, levels, land, masks, *weights)
 
 
-def hand_out_kernel(new_in, node_in, edge_in, packed, new_nodes, node_grad, edge_grad, *rest):
-    outs, sems = rest[:-1], rest[-1]
-    copies = [
-        pltpu.make_async_copy(src, dst, sems.at[k])
-        for k, (src, dst) in enumerate(
-            ((edge_in, edge_grad), (new_in, new_nodes), (node_in, node_grad))
-        )
-    ]
-    for copy in copies:
+def hand_out_kernel(edge_in, new_in, node_in, packed, edge_grad, new_nodes, node_grad, *rest):
+    outs, (hold_edge, hold_new, hold_node, sems) = rest[:-4], rest[-4:]
+    parts = []
+    cuts = sems.shape[1] - 2
+    wide = edge_in.shape[1] // cuts
+    for c in range(cuts):
+        here = pl.ds(c * wide, wide)
+        parts.append((edge_in.at[:, here], hold_edge.at[:, here], edge_grad.at[:, here]))
+    parts.append((new_in, hold_new, new_nodes))
+    parts.append((node_in, hold_node, node_grad))
+    ins = [pltpu.make_async_copy(a, b, sems.at[0, k]) for k, (a, b, _) in enumerate(parts)]
+    backs = [pltpu.make_async_copy(b, c, sems.at[1, k]) for k, (_, b, c) in enumerate(parts)]
+    for copy in ins:
         copy.start()
     rows = packed.shape[1] // 2
     lines = packed[3 * rows :, :].T
@@ -702,31 +700,36 @@
     node_second[...] = packed[2 * rows : 3 * rows, rows:]
     for k, out in enumerate((edge_b1, edge_b2, edge_g, edge_h, node_b1, node_b2, node_g, node_h)):
         out[...] = lines[k, :rows]
-    for copy in copies:
+    for copy, back in zip(ins, backs):
         copy.wait()
+        back.start()
+    for back in backs:
+        back.wait()
 
 
 def hand_out(new_nodes, node_grad, edge_grad, packed):
     rows = packed.shape[1] // 2
+    cuts = 4
     vmem = pl.BlockSpec(memory_space=pltpu.VMEM)
     stay = pl.BlockSpec(memory_space=pl.ANY)
     shapes = [
         (rows, 3 * rows), (rows,), (rows, rows), (rows,), (rows,), (rows,),
         (rows, 2 * rows), (rows,), (rows, rows), (rows,), (rows,), (rows,),
     ]
-    large = [jax.ShapeDtypeStruct(a.shape, a.dtype) for a in (new_nodes, node_grad, edge_grad)]
-    outs = pl.pallas_call(
+    large = (edge_grad, new_nodes, node_grad)
+    edge_grad, new_nodes, node_grad, *small = pl.pallas_call(
         hand_out_kernel,
         in_specs=[stay] * 3 + [vmem],
         out_specs=[stay] * 3 + [vmem] * len(shapes),
-        out_shape=large + [jax.ShapeDtypeStruct(s, F32) for s in shapes],
-        scratch_shapes=[pltpu.SemaphoreType.DMA((3,))],
+        out_shape=[jax.ShapeDtypeStruct(a.shape, a.dtype) for a in large]
+        + [jax.ShapeDtypeStruct(s, F32) for s in shapes],
+        scratch_shapes=[pltpu.VMEM(a.shape, a.dtype) for a in large]
+        + [pltpu.SemaphoreType.DMA((2, cuts + 2))],
         compiler_params=pltpu.CompilerParams(vmem_limit_bytes=VMEM_LIMIT),
         name="hand_out",
-    )(new_nodes, node_grad, edge_grad, packed)
-    outs = list(outs)
-    outs[3], outs[9] = outs[3].T, outs[9].T
-    return tuple(outs)
+    )(*large, packed)
+    small[0], small[6] = small[0].T, small[6].T
+    return (new_nodes, node_grad, edge_grad, *small)
 
 
 def per_device(

time: 314 us -> 192 us (0.61)
  Pallas kernels: 313 us -> 191 us
    pallas_call x1, Pallas kernels: 98 us -> 4.4 us  [hand_out(): pl.pallas_call(hand_out_kernel, in_specs=[stay] * 3 + [vmem], out_specs=[...]
    pallas_call x1, Pallas kernels: 215 us -> 186 us  [layer(): pl.pallas_call(functools.partial(layer_kernel, masks.shape[0], reps), in_...]
where the time goes in v4:
time: 192 us; the launch traced here: 191 us
  Pallas kernels  191 us (99%)
    pallas_call x1, Pallas kernels, layer(): pl.pallas_call(functools.partial(layer_kernel, masks.shape[0], reps), in_...  186 us
    pallas_call x1, Pallas kernels, hand_out(): pl.pallas_call(hand_out_kernel, in_specs=[stay] * 3 + [vmem], out_specs=[...  4.4 us

profile of v4, /device:TPU:0, one launch (start us, length us, event | category | flops | bytes accessed | tf_op | source)
XLA Modules:
  0.0 191.4 jit_solution(7523696298129246062)
XLA Ops:
  0.7 186.2 %layer.1 = (bf16[64,4096]{1,0:T(8,128)(2,1)}, bf16[64,4096]{1,0:T(8,128)(2,1)}, bf16[64,16384]{1,0:T(8,128)(2,1)}, f32[256,128]{1,0:T(8,128)}) custom-call(s32[16]{0:T(128)} %counts.1, bf16[64,4096]{1,0:T(8,128)(2,1)} %nodes.1, bf16[64,16384]{1,0:T(8,128)(2,1)} %edges.1, bf16[64,4096]{1,0:T(8,128)(2,1)} %target.1, s32[16,1,1024]{2,1,0:T(1,128)} %bitcast.8, ...), custom_call_target="tpu_custom_call" | custom-call | flops 68719476736 | bytes 16777216 | tf_op jit(solution)/shard_map/layer/pallas_call | solution.py:619
  186.8 4.4 %hand_out.1 = (bf16[64,16384]{1,0:T(8,128)(2,1)}, bf16[64,4096]{1,0:T(8,128)(2,1)}, bf16[64,4096]{1,0:T(8,128)(2,1)}, f32[64,192]{1,0:T(8,128)}, f32[64]{0:T(128...) custom-call(bf16[64,16384]{1,0:T(8,128)(2,1)} %get-tuple-element.34., ...), custom_call_target="tpu_custom_call" | custom-call | tf_op jit(solution)/shard_map/hand_out/pallas_call | solution.py:720
